TPU v7x, 32 devices: a whole 2x2x4 slice. The times are simulated.
32 devices in a mesh: dp: 8 (over z, y), tensor: 4 (over x, core).
Axes of the slice: x: 2, y: 2, z: 4, core: 2. Of those that a mesh axis runs over, the one named last changes fastest.
Arguments:
- band_patches: bfloat16 [64, 13, 256, 768], P('dp', None, 'tensor'), may hold values from -6 to 6
- band_counts: int32 [64], P('dp'), may hold values from 4 to 13
- visible_index: int32 [64, 64], P('dp'), may hold values from 0 to 255, as said below
- enc_attn_gain: float32 [768], replicated, may hold values from 0.5 to 1.5
- enc_attn_shift: float32 [768], replicated, may hold values from -1.75 to 1.75
- enc_qkv_weight: bfloat16 [3, 768, 768], P(None, 'tensor'), may hold values from -0.21875 to 0.21875
- enc_out_weight: bfloat16 [768, 768], P('tensor'), may hold values from -1.75 to 1.75
- enc_out_bias: float32 [768], replicated, may hold values from -1.75 to 1.75
- enc_mlp_gain: float32 [768], replicated, may hold values from 0.5 to 1.5
- enc_mlp_shift: float32 [768], replicated, may hold values from -1.75 to 1.75
- enc_up_weight: bfloat16 [768, 3072], P(None, 'tensor'), may hold values from -0.21875 to 0.21875
- enc_up_bias: float32 [3072], P('tensor'), may hold values from -3 to 3
- enc_down_weight: bfloat16 [3072, 768], P('tensor'), may hold values from -0.109375 to 0.109375
- enc_down_bias: float32 [768], replicated, may hold values from -1.75 to 1.75
- proj_weight: bfloat16 [768, 512], replicated, may hold values from -0.21875 to 0.21875
- proj_bias: float32 [512], replicated, may hold values from -1.75 to 1.75
- mask_token: float32 [512], replicated, may hold values from -6 to 6
- dec_attn_gain: float32 [512], replicated, may hold values from 0.5 to 1.5
- dec_attn_shift: float32 [512], replicated, may hold values from -1.75 to 1.75
- dec_qkv_weight: bfloat16 [3, 256, 512], P(None, 'tensor'), may hold values from -0.25 to 0.25
- dec_out_weight: bfloat16 [256, 512], P('tensor'), may hold values from -6 to 6
- dec_out_bias: float32 [512], replicated, may hold values from -1.75 to 1.75
- dec_mlp_gain: float32 [512], replicated, may hold values from 0.5 to 1.5
- dec_mlp_shift: float32 [512], replicated, may hold values from -1.75 to 1.75
- dec_up_weight: bfloat16 [512, 2048], P(None, 'tensor'), may hold values from -0.25 to 0.25
- dec_up_bias: float32 [2048], replicated, may hold values from -3 to 3
- dec_down_weight: bfloat16 [2048, 512], P('tensor'), may hold values from -0.125 to 0.125
- dec_down_bias: float32 [512], replicated, may hold values from -1.75 to 1.75
- cotangent: bfloat16 [64, 256, 512], P('dp'), may hold values from -8 to 8
Outputs:
- decoded: float32 [64, 256, 512], P('dp', None, 'tensor')
- band_grad: float32 [64, 13, 256, 768], P('dp', None, 'tensor')
- grad_enc_attn_gain: float32 [768], P('dp')
- grad_enc_attn_shift: float32 [768], P('dp')
- grad_enc_qkv_weight: float32 [3, 768, 768], P(None, 'tensor', 'dp')
- grad_enc_out_weight: float32 [768, 768], P('tensor', 'dp')
- grad_enc_out_bias: float32 [768], P('dp')
- grad_enc_mlp_gain: float32 [768], P('dp')
- grad_enc_mlp_shift: float32 [768], P('dp')
- grad_enc_up_weight: float32 [768, 3072], P('dp', 'tensor')
- grad_enc_up_bias: float32 [3072], P(('tensor', 'dp'))
- grad_enc_down_weight: float32 [3072, 768], P('tensor', 'dp')
- grad_enc_down_bias: float32 [768], P('dp')
- grad_proj_weight: float32 [768, 512], P('dp')
- grad_proj_bias: float32 [512], P('dp')
- grad_mask_token: float32 [512], P('dp')
- grad_dec_attn_gain: float32 [512], P('dp')
- grad_dec_attn_shift: float32 [512], P('dp')
- grad_dec_qkv_weight: float32 [3, 256, 512], P(None, 'tensor', 'dp')
- grad_dec_out_weight: float32 [256, 512], P('tensor', 'dp')
- grad_dec_out_bias: float32 [512], P('dp')
- grad_dec_mlp_gain: float32 [512], P('dp')
- grad_dec_mlp_shift: float32 [512], P('dp')
- grad_dec_up_weight: float32 [512, 2048], P('dp', 'tensor')
- grad_dec_up_bias: float32 [2048], P(('tensor', 'dp'))
- grad_dec_down_weight: float32 [2048, 512], P('tensor', 'dp')
- grad_dec_down_bias: float32 [512], P('dp')
Inputs may be any that keep to these rules, and one draw needn't show every extreme that they name: `visible_index`: each row holds 64 different patch numbers in rising order.
All inputs are finite; a program needn't handle non-finite values.
Results may differ from a plain program's by a relative error of at most 0.029.
Values may be sent and summed in bfloat16 or wider, within the bound.
No kernel may reach another device: no remote copies, remote signals or barrier semaphores. Data moves between devices by JAX's collectives and lax.ppermute only.
A program may use at most 192 MiB of HBM per device.

v0:
```python
import math

import jax
import jax.numpy as jnp
from jax import lax
from jax.sharding import PartitionSpec as P

HEAD = 64


EPSILON = 1e-05


def layer_norm(stream, gain, shift):
    center = stream - jnp.mean(stream, -1, keepdims=True)
    inverse = lax.rsqrt(jnp.mean(center * center, -1, keepdims=True) + EPSILON)
    return center * inverse * gain + shift


def exact_gelu(values):
    return jax.nn.gelu(values, approximate=False)


def sincos_table(count, width):
    places = lax.broadcasted_iota(jnp.float32, (count, width // 2), 0)
    orders = lax.broadcasted_iota(jnp.float32, (count, width // 2), 1)
    angles = places * jnp.exp(orders * (-math.log(10000.0) / (width // 2)))
    return jnp.concatenate([jnp.sin(angles), jnp.cos(angles)], 1)


def split_heads(qkv_low):
    chip_count, length, _, inner_width = qkv_low.shape
    shaped = qkv_low.reshape(chip_count, length, 3, inner_width // HEAD, HEAD)
    return (shaped[:, :, 0], shaped[:, :, 1], shaped[:, :, 2])


def score_block(queries, keyset):
    raw_scores = jnp.einsum("cqhe,ckhe->chqk", queries, keyset, preferred_element_type=jnp.float32)
    return raw_scores * HEAD ** (-0.5)


def attn_sum(partial_out, sum_kind):
    if sum_kind == "enc":
        return lax.psum(partial_out, "tensor")
    return lax.psum(partial_out, "tensor")


def mlp_sum(partial_down, sum_kind):
    if sum_kind == "enc":
        return lax.psum(partial_down, "tensor")
    return lax.psum(partial_down.astype(jnp.bfloat16), "tensor").astype(jnp.float32)


def mlp_back_sum(partial_grad, sum_kind):
    if sum_kind == "enc":
        return lax.psum(partial_grad.astype(jnp.bfloat16), "tensor").astype(jnp.float32)
    return lax.psum(partial_grad.astype(jnp.bfloat16), "tensor").astype(jnp.float32)


def attn_back_sum(partial_grad, sum_kind):
    if sum_kind == "enc":
        return lax.psum(partial_grad.astype(jnp.bfloat16), "tensor").astype(jnp.float32)
    return lax.psum(partial_grad, "tensor")


def block_forward(stream, params, sum_kind):
    (
        attn_gain,
        attn_shift,
        qkv_weight,
        out_weight,
        out_bias,
        mlp_gain,
        mlp_shift,
        up_weight,
        up_bias,
        down_weight,
        down_bias,
    ) = params
    normed = layer_norm(stream, attn_gain, attn_shift).astype(jnp.bfloat16)
    qkv_low = jnp.einsum(
        "csd,tid->csti", normed, qkv_weight, preferred_element_type=jnp.float32
    ).astype(jnp.bfloat16)
    queries, keyset, valset = split_heads(qkv_low)
    scores = score_block(queries, keyset)
    log_total = jax.nn.logsumexp(scores, -1, keepdims=True)
    prob_low = jnp.exp(scores - log_total).astype(jnp.bfloat16)
    mixed_rows = jnp.einsum("chqk,ckhe->cqhe", prob_low, valset, preferred_element_type=jnp.float32)
    mixed_low = mixed_rows.reshape(mixed_rows.shape[0], mixed_rows.shape[1], -1).astype(
        jnp.bfloat16
    )
    partial_out = jnp.einsum(
        "csi,id->csd", mixed_low, out_weight, preferred_element_type=jnp.float32
    )
    middle = stream + attn_sum(partial_out, sum_kind) + out_bias
    mlp_normed = layer_norm(middle, mlp_gain, mlp_shift).astype(jnp.bfloat16)
    hidden = (
        jnp.einsum("csd,df->csf", mlp_normed, up_weight, preferred_element_type=jnp.float32)
        + up_bias
    )
    act_low = exact_gelu(hidden).astype(jnp.bfloat16)
    partial_down = jnp.einsum(
        "csf,fd->csd", act_low, down_weight, preferred_element_type=jnp.float32
    )
    result = middle + mlp_sum(partial_down, sum_kind) + down_bias
    return (result, (stream, middle, qkv_low, log_total, mixed_low))


def block_backward(grad_out, saved, params, sum_kind):
    (
        attn_gain,
        attn_shift,
        qkv_weight,
        out_weight,
        out_bias,
        mlp_gain,
        mlp_shift,
        up_weight,
        up_bias,
        down_weight,
        down_bias,
    ) = params
    stream, middle, qkv_low, log_total, mixed_low = saved
    chip_count, length, _, inner_width = qkv_low.shape
    mlp_normed, mlp_norm_back = jax.vjp(layer_norm, middle, mlp_gain, mlp_shift)
    normed_low = mlp_normed.astype(jnp.bfloat16)
    hidden = (
        jnp.einsum("csd,df->csf", normed_low, up_weight, preferred_element_type=jnp.float32)
        + up_bias
    )
    activation, gelu_back = jax.vjp(exact_gelu, hidden)
    act_low = activation.astype(jnp.bfloat16)
    grad_low = grad_out.astype(jnp.bfloat16)
    grad_down_bias = jnp.sum(grad_out, (0, 1))
    grad_down_weight = jnp.einsum(
        "csf,csd->fd", act_low, grad_low, preferred_element_type=jnp.float32
    )
    grad_act = jnp.einsum("csd,fd->csf", grad_low, down_weight, preferred_element_type=jnp.float32)
    grad_hidden = gelu_back(grad_act)[0]
    grad_up_bias = jnp.sum(grad_hidden, (0, 1))
    hidden_low = grad_hidden.astype(jnp.bfloat16)
    grad_up_weight = jnp.einsum(
        "csd,csf->df", normed_low, hidden_low, preferred_element_type=jnp.float32
    )
    grad_mlp_normed = mlp_back_sum(
        jnp.einsum("csf,df->csd", hidden_low, up_weight, preferred_element_type=jnp.float32),
        sum_kind,
    )
    grad_middle_norm, grad_mlp_gain, grad_mlp_shift = mlp_norm_back(grad_mlp_normed)
    grad_middle = grad_out + grad_middle_norm
    middle_low = grad_middle.astype(jnp.bfloat16)
    grad_out_bias = jnp.sum(grad_middle, (0, 1))
    grad_out_weight = jnp.einsum(
        "csi,csd->id", mixed_low, middle_low, preferred_element_type=jnp.float32
    )
    grad_mixed = jnp.einsum(
        "csd,id->csi", middle_low, out_weight, preferred_element_type=jnp.float32
    ).astype(jnp.bfloat16)
    grad_mixed = grad_mixed.reshape(chip_count, length, inner_width // HEAD, HEAD)
    queries, keyset, valset = split_heads(qkv_low)
    prob_full = jnp.exp(score_block(queries, keyset) - log_total)
    prob_low = prob_full.astype(jnp.bfloat16)
    grad_probs = jnp.einsum(
        "cqhe,ckhe->chqk", grad_mixed, valset, preferred_element_type=jnp.float32
    )
    grad_values = jnp.einsum(
        "chqk,cqhe->ckhe", prob_low, grad_mixed, preferred_element_type=jnp.float32
    )
    grad_scores = prob_full * (grad_probs - jnp.sum(grad_probs * prob_full, -1, keepdims=True))
    score_low = grad_scores.astype(jnp.bfloat16)
    grad_queries = jnp.einsum(
        "chqk,ckhe->cqhe", score_low, keyset, preferred_element_type=jnp.float32
    ) * HEAD ** (-0.5)
    grad_keys = jnp.einsum(
        "chqk,cqhe->ckhe", score_low, queries, preferred_element_type=jnp.float32
    ) * HEAD ** (-0.5)
    grad_qkv = (
        jnp.stack([grad_queries, grad_keys, grad_values], 2)
        .reshape(chip_count, length, 3, inner_width)
        .astype(jnp.bfloat16)
    )
    attn_normed, attn_norm_back = jax.vjp(layer_norm, stream, attn_gain, attn_shift)
    attn_low = attn_normed.astype(jnp.bfloat16)
    grad_qkv_weight = jnp.einsum(
        "csd,csti->tid", attn_low, grad_qkv, preferred_element_type=jnp.float32
    )
    grad_attn_normed = attn_back_sum(
        jnp.einsum("csti,tid->csd", grad_qkv, qkv_weight, preferred_element_type=jnp.float32),
        sum_kind,
    )
    grad_stream_norm, grad_attn_gain, grad_attn_shift = attn_norm_back(grad_attn_normed)
    grad_stream = grad_middle + grad_stream_norm
    grad_list = (
        grad_attn_gain,
        grad_attn_shift,
        grad_qkv_weight,
        grad_out_weight,
        grad_out_bias,
        grad_mlp_gain,
        grad_mlp_shift,
        grad_up_weight,
        grad_up_bias,
        grad_down_weight,
        grad_down_bias,
    )
    return (grad_stream, grad_list)


def body(
    band_patches,
    band_counts,
    visible_index,
    enc_attn_gain,
    enc_attn_shift,
    enc_qkv_weight,
    enc_out_weight,
    enc_out_bias,
    enc_mlp_gain,
    enc_mlp_shift,
    enc_up_weight,
    enc_up_bias,
    enc_down_weight,
    enc_down_bias,
    proj_weight,
    proj_bias,
    mask_token,
    dec_attn_gain,
    dec_attn_shift,
    dec_qkv_weight,
    dec_out_weight,
    dec_out_bias,
    dec_mlp_gain,
    dec_mlp_shift,
    dec_up_weight,
    dec_up_bias,
    dec_down_weight,
    dec_down_bias,
    cotangent,
):
    enc_params = (
        enc_attn_gain,
        enc_attn_shift,
        enc_qkv_weight,
        enc_out_weight,
        enc_out_bias,
        enc_mlp_gain,
        enc_mlp_shift,
        enc_up_weight,
        enc_up_bias,
        enc_down_weight,
        enc_down_bias,
    )
    chip_count = band_counts.shape[0]
    band_total = band_patches.shape[1]
    own_patches = band_patches.shape[2]
    enc_width = band_patches.shape[3]
    patches = cotangent.shape[1]
    dec_width = cotangent.shape[2]
    group_size = lax.axis_size("tensor")
    tensor_rank = lax.axis_index("tensor")
    band_used = (
        lax.broadcasted_iota(jnp.int32, (chip_count, band_total), 1) < band_counts[:, None]
    ).astype(jnp.float32)
    counts_float = band_counts.astype(jnp.float32)[:, None, None]
    own_mean = (
        jnp.einsum(
            "cb,cbpd->cpd",
            band_used.astype(jnp.bfloat16),
            band_patches,
            preferred_element_type=jnp.float32,
        )
        / counts_float
    )
    all_mean = lax.all_gather(own_mean.astype(jnp.bfloat16), "tensor", axis=1, tiled=True)
    tokens = jnp.take_along_axis(all_mean, visible_index[:, :, None], axis=1).astype(jnp.float32)
    enc_out, enc_saved = block_forward(tokens, enc_params, "enc")
    enc_low = enc_out.astype(jnp.bfloat16)
    latent = (
        jnp.einsum("cvd,de->cve", enc_low, proj_weight, preferred_element_type=jnp.float32)
        + proj_bias
    )
    chip_rows = lax.broadcasted_iota(jnp.int32, visible_index.shape, 0)
    position_table = sincos_table(patches, dec_width)
    decoder_in = (
        jnp.broadcast_to(mask_token, cotangent.shape).at[chip_rows, visible_index].set(latent)
        + position_table
    )
    is_visible = jnp.zeros((chip_count, patches), jnp.float32).at[chip_rows, visible_index].set(1.0)
    column_count = dec_width // group_size
    own_hidden = dec_up_weight.shape[1]
    bias_share = lax.dynamic_slice_in_dim(dec_up_bias, tensor_rank * own_hidden, own_hidden, 0)
    dec_params = (
        dec_attn_gain,
        dec_attn_shift,
        dec_qkv_weight,
        dec_out_weight,
        dec_out_bias,
        dec_mlp_gain,
        dec_mlp_shift,
        dec_up_weight,
        bias_share,
        dec_down_weight,
        dec_down_bias,
    )
    decoded_full, dec_saved = block_forward(decoder_in, dec_params, "dec")
    decoded = lax.dynamic_slice_in_dim(decoded_full, tensor_rank * column_count, column_count, 2)
    grad_decoder_in, dec_grads = block_backward(
        cotangent.astype(jnp.float32), dec_saved, dec_params, "dec"
    )
    grad_mask_token = jnp.sum((1.0 - is_visible)[:, :, None] * grad_decoder_in, (0, 1))
    grad_latent = jnp.take_along_axis(grad_decoder_in, visible_index[:, :, None], axis=1)
    grad_proj_bias = jnp.sum(grad_latent, (0, 1))
    latent_low = grad_latent.astype(jnp.bfloat16)
    grad_proj_weight = jnp.einsum(
        "cvd,cve->de", enc_low, latent_low, preferred_element_type=jnp.float32
    )
    grad_enc_out = jnp.einsum(
        "cve,de->cvd", latent_low, proj_weight, preferred_element_type=jnp.float32
    )
    grad_tokens, enc_grads = block_backward(grad_enc_out, enc_saved, enc_params, "enc")
    grad_mean = (
        jnp.zeros((chip_count, patches, enc_width), jnp.float32)
        .at[chip_rows, visible_index]
        .set(grad_tokens / counts_float)
    )
    grad_own = lax.dynamic_slice_in_dim(grad_mean, tensor_rank * own_patches, own_patches, 1)
    band_grad = band_used[:, :, None, None] * grad_own[:, None]
    all_shares = (
        lax.psum_scatter(enc_grads[0], "dp", scatter_dimension=0, tiled=True),
        lax.psum_scatter(enc_grads[1], "dp", scatter_dimension=0, tiled=True),
        lax.psum_scatter(enc_grads[2], "dp", scatter_dimension=2, tiled=True),
        lax.psum_scatter(enc_grads[3], "dp", scatter_dimension=1, tiled=True),
        lax.psum_scatter(enc_grads[4], "dp", scatter_dimension=0, tiled=True),
        lax.psum_scatter(enc_grads[5], "dp", scatter_dimension=0, tiled=True),
        lax.psum_scatter(enc_grads[6], "dp", scatter_dimension=0, tiled=True),
        lax.psum_scatter(enc_grads[7], "dp", scatter_dimension=0, tiled=True),
        lax.psum_scatter(enc_grads[8], "dp", scatter_dimension=0, tiled=True),
        lax.psum_scatter(enc_grads[9], "dp", scatter_dimension=1, tiled=True),
        lax.psum_scatter(enc_grads[10], "dp", scatter_dimension=0, tiled=True),
        lax.psum_scatter(dec_grads[0], "dp", scatter_dimension=0, tiled=True),
        lax.psum_scatter(dec_grads[1], "dp", scatter_dimension=0, tiled=True),
        lax.psum_scatter(dec_grads[2], "dp", scatter_dimension=2, tiled=True),
        lax.psum_scatter(dec_grads[3], "dp", scatter_dimension=1, tiled=True),
        lax.psum_scatter(dec_grads[4], "dp", scatter_dimension=0, tiled=True),
        lax.psum_scatter(dec_grads[5], "dp", scatter_dimension=0, tiled=True),
        lax.psum_scatter(dec_grads[6], "dp", scatter_dimension=0, tiled=True),
        lax.psum_scatter(dec_grads[7], "dp", scatter_dimension=0, tiled=True),
        lax.psum_scatter(dec_grads[8], "dp", scatter_dimension=0, tiled=True),
        lax.psum_scatter(dec_grads[9], "dp", scatter_dimension=1, tiled=True),
        lax.psum_scatter(dec_grads[10], "dp", scatter_dimension=0, tiled=True),
        lax.psum_scatter(grad_proj_weight, "dp", scatter_dimension=0, tiled=True),
        lax.psum_scatter(grad_proj_bias, "dp", scatter_dimension=0, tiled=True),
        lax.psum_scatter(grad_mask_token, "dp", scatter_dimension=0, tiled=True),
    )
    enc_shares = all_shares[:11]
    dec_shares = all_shares[11:]
    return (
        decoded,
        band_grad,
        enc_shares[0],
        enc_shares[1],
        enc_shares[2],
        enc_shares[3],
        enc_shares[4],
        enc_shares[5],
        enc_shares[6],
        enc_shares[7],
        enc_shares[8],
        enc_shares[9],
        enc_shares[10],
        dec_shares[11],
        dec_shares[12],
        dec_shares[13],
        dec_shares[0],
        dec_shares[1],
        dec_shares[2],
        dec_shares[3],
        dec_shares[4],
        dec_shares[5],
        dec_shares[6],
        dec_shares[7],
        dec_shares[8],
        dec_shares[9],
        dec_shares[10],
    )


def solution(mesh):
    in_specs = (
        P("dp", None, "tensor", None),
        P("dp"),
        P("dp", None),
        P(),
        P(),
        P(None, "tensor", None),
        P("tensor", None),
        P(),
        P(),
        P(),
        P(None, "tensor"),
        P("tensor"),
        P("tensor", None),
        P(),
        P(),
        P(),
        P(),
        P(),
        P(),
        P(None, "tensor", None),
        P("tensor", None),
        P(),
        P(),
        P(),
        P(None, "tensor"),
        P(),
        P("tensor", None),
        P(),
        P("dp", None, None),
    )
    out_specs = (
        P("dp", None, "tensor"),
        P("dp", None, "tensor", None),
        P("dp"),
        P("dp"),
        P(None, "tensor", "dp"),
        P("tensor", "dp"),
        P("dp"),
        P("dp"),
        P("dp"),
        P("dp", "tensor"),
        P(("tensor", "dp")),
        P("tensor", "dp"),
        P("dp"),
        P("dp", None),
        P("dp"),
        P("dp"),
        P("dp"),
        P("dp"),
        P(None, "tensor", "dp"),
        P("tensor", "dp"),
        P("dp"),
        P("dp"),
        P("dp"),
        P("dp", "tensor"),
        P(("tensor", "dp")),
        P("tensor", "dp"),
        P("dp"),
    )
    return jax.shard_map(body, mesh=mesh, in_specs=in_specs, out_specs=out_specs, check_vma=False)
```

profile of v0, /device:TPU:0, one launch (start us, length us, event | category | flops | bytes accessed | tf_op | source)
XLA Modules:
  0.0 1274.0 jit_solution(15353857982112573844)
XLA Ops:
  9.3 10.1 fusion
  21.3 30.6 %all-gather.2.cloned.1.call-done = bf16[8,256,768]{2,1,0:T(8,128)(2,1)} async-done(((bf16[8,64,768]{2,1,0:T(8,128)(2,1)}), bf16[8,256,768]{2,1,0:T(8,128)(2,1)}) %all-gather.2.cloned.1.call-update) | async-done | bytes 3145744 | tf_op jit(solution)/shard_map/all_gather | solution.py:274
  51.9 7.6 gather_fusion
  70.1 42.8 %all-reduce.26.cloned.1.call-done = f32[8,64,768]{2,1,0:T(8,128)} async-done(((f32[8,64,768]{2,1,0:T(8,128)}), f32[8,64,768]{2,1,0:T(8,128)}) %all-reduce.26.cloned.1.call-update) | async-done | bytes 1572880 | tf_op jit(solution)/shard_map/psum | solution.py:44
  130.1 40.4 %all-reduce.28.cloned.1.call-done = f32[8,64,768]{2,1,0:T(8,128)} async-done(((f32[8,64,768]{2,1,0:T(8,128)}), f32[8,64,768]{2,1,0:T(8,128)}) %all-reduce.28.cloned.1.call-update) | async-done | bytes 1572880 | tf_op jit(solution)/shard_map/psum | solution.py:50
  177.0 64.5 %scatter_fusion = f32[8,256,512]{2,1,0:T(8,128)} fusion(f32[8,256,512]{2,1,0:T(8,128)} %broadcast_in_dim.42, s32[512]{0:T(512)S(1)} %reshape.386, f32[512,512]{1,0:T(8,128)} %bitcast.278), kind=kCustom, calls=%fused_computation.2 | custom fusion | bytes 3149824 | tf_op jit(solution)/shard_map/scatter | solution.py:285
  254.9 84.3 %all-reduce.30.cloned.1.call-done = f32[8,256,512]{2,1,0:T(8,128)} async-done(((f32[8,256,512]{2,1,0:T(8,128)}), f32[8,256,512]{2,1,0:T(8,128)}) %all-reduce.30.cloned.1.call-update) | async-done | bytes 4194320 | tf_op jit(solution)/shard_map/psum | solution.py:45
  348.1 10.3 multiply_convert_fusion
  366.1 51.2 %all-reduce.32.cloned.1.call-done = bf16[8,256,512]{2,1,0:T(8,128)(2,1)} async-done(((bf16[8,256,512]{2,1,0:T(8,128)(2,1)}), bf16[8,256,512]{2,1,0:T(8,128)(2,1)}) %all-reduce.32.cloned.1.call-update) | async-done | bytes 2097168 | tf_op jit(solution)/shard_map/psum | solution.py:57
  439.8 42.4 %scatter_fusion.2 = f32[8,256]{1,0:T(8,128)S(1)} fusion(f32[8,256]{1,0:T(8,128)S(1)} %broadcast_in_dim.47, s32[512]{0:T(512)S(1)} %reshape.386, f32[512]{0:T(512)} %broadcast.588), kind=kCustom, calls=%fused_computation.4 | custom fusion | bytes 10240 | tf_op jit(solution)/shard_map/scatter | solution.py:288
  482.8 41.9 %all-reduce.34.cloned.1.call-done = f32[8,256,512]{2,1,0:T(8,128)} async-done(((f32[8,256,512]{2,1,0:T(8,128)}), f32[8,256,512]{2,1,0:T(8,128)}) %all-reduce.34.cloned.1.call-update) | async-done | bytes 4194320 | tf_op jit(solution)/shard_map/psum | solution.py:63
  537.7 9.3 gather_fusion.1
  571.4 19.1 %all-reduce.36.cloned.1.call-done = bf16[8,64,768]{2,1,0:T(8,128)(2,1)} async-done(((bf16[8,64,768]{2,1,0:T(8,128)(2,1)}), bf16[8,64,768]{2,1,0:T(8,128)(2,1)}) %all-reduce.36.cloned.1.call-update) | async-done | bytes 786448 | tf_op jit(solution)/shard_map/psum | solution.py:56
  643.3 5.9 convolution_bitcast_fusion.6
  671.3 48.9 %reduce-scatter.32.cloned.1.call-done = f32[64,192]{1,0:T(8,128)} async-done(((f32[512,192]{1,0:T(8,128)}), f32[64,192]{1,0:T(8,128)}) %reduce-scatter.32.cloned.1.call-update) | async-done | bytes 49168
  722.6 62.2 %reduce-scatter.30.cloned.1.call-done = f32[96,192]{1,0:T(8,128)} async-done(((f32[768,192]{1,0:T(8,128)}), f32[96,192]{1,0:T(8,128)}) %reduce-scatter.30.cloned.1.call-update) | async-done | bytes 73744
  786.4 64.4 %all-reduce.38.cloned.1.call-done = (bf16[8,256,512]{2,1,0:T(8,128)(2,1)}, bf16[8,64,768]{2,1,0:T(8,128)(2,1)}) async-done(((bf16[8,256,512]{2,1,0:T(8,128)(2,1)}, bf16[8,64,768]{2,1,0:T(8,128)(2,1)}), (bf16[8,256,512]{2,1,0:T(8,128)(2,1)}, bf16[8,64,768]{2,1,0:T(8,128)(2,1)})) %all-reduce.38.cloned.1.call-update) | async-done | bytes 2883600 | tf_op jit(solution)/shard_map/psum | solution.py:51
  857.4 39.1 %all-reduce.16 = (f32[768]{0:T(1024)}, f32[768]{0:T(1024)}, f32[768]{0:T(1024)}, f32[768]{0:T(1024)}, f32[768]{0:T(1024)}, /*index=5*/f32[768]{0:T(1024)}, f32[7...) all-reduce(f32[768]{0:T(1024)} %get-tuple-element.41, ...), channel_id=2, replica_groups=mesh['dp'=8,'tensor'=4] {'dp'}, use_global_device_ids=true, to_apply=%region_33.34.clone | all-reduce | flops 9984 | bytes 79872
  923.3 69.8 %scatter_fusion.1 = f32[8,256,768]{2,1,0:T(8,128)} fusion(f32[8,256,768]{2,1,0:T(8,128)} %broadcast_in_dim.48, s32[512]{0:T(512)S(1)} %reshape.386, f32[512,768]{1,0:T(8,128)S(1)} %bitcast.266), kind=kCustom, calls=%fused_computation.3 | custom fusion | bytes 4722688 | tf_op jit(solution)/shard_map/scatter | solution.py:324
  997.1 10.0 broadcast_multiply_fusion
  1009.1 45.6 %reduce-scatter.26.cloned.1.call-done = f32[512,64]{0,1:T(8,128)} async-done(((f32[512,512]{0,1:T(8,128)}), f32[512,64]{0,1:T(8,128)}) %reduce-scatter.26.cloned.1.call-update) | async-done | bytes 131088 | tf_op jit(solution)/shard_map/reduce_scatter | solution.py:349
  1054.7 67.8 %reduce-scatter.22.cloned.1.call-done = f32[96,512]{1,0:T(8,128)} async-done(((f32[768,512]{1,0:T(8,128)}), f32[96,512]{1,0:T(8,128)}) %reduce-scatter.22.cloned.1.call-update) | async-done | bytes 196624 | tf_op jit(solution)/shard_map/reduce_scatter | solution.py:351
  1122.5 72.0 %reduce-scatter.18.cloned.1.call-done = f32[96,768]{1,0:T(8,128)} async-done(((f32[768,768]{1,0:T(8,128)}), f32[96,768]{1,0:T(8,128)}) %reduce-scatter.18.cloned.1.call-update) | async-done | bytes 294928 | tf_op jit(solution)/shard_map/reduce_scatter | solution.py:336
  1194.5 72.5 %reduce-scatter.20.cloned.1.call-done = f32[768,96]{0,1:T(8,128)} async-done(((f32[768,768]{0,1:T(8,128)}), f32[768,96]{0,1:T(8,128)}) %reduce-scatter.20.cloned.1.call-update) | async-done | bytes 294928 | tf_op jit(solution)/shard_map/reduce_scatter | solution.py:338
  (389 shorter events, 244.6 us)
Async XLA Ops:
  7.2 109.7 %copy-start = (bf16[768,768]{1,0:T(8,128)(2,1)S(1)}, bf16[768,768]{1,0:T(8,128)(2,1)}, u32[]{:S(2)}) copy-start(bf16[768,768]{1,0:T(8,128)(2,1)} %param.39) | copy-start | bytes 3538948
  7.2 44.7 %all-gather.2.cloned.1.call-start = ((), (), s32[]{:S(2)}) async-start(), calls=%async_computation.9 | async-start | bytes 3932160 | tf_op jit(solution)/shard_map/all_gather | solution.py:274
  20.5 92.4 %all-reduce.26.cloned.1.call-start = ((), (), s32[]{:S(2)}) async-start(), calls=%async_computation.10 | async-start | bytes 3145728 | tf_op jit(solution)/shard_map/psum | solution.py:44
  21.3 149.2 %copy-start.54 = (pred[8,64]{1,0:T(8,128)(4,1)}, pred[8,64]{1,0:T(8,128)(4,1)S(1)}, u32[]{:S(2)}) copy-start(pred[8,64]{1,0:T(8,128)(4,1)S(1)} %compare_and_fusion) | copy-start | bytes 1540
  69.9 100.6 %all-reduce.28.cloned.1.call-start = ((), (), s32[]{:S(2)}) async-start(), calls=%async_computation.11 | async-start | bytes 3145728 | tf_op jit(solution)/shard_map/psum | solution.py:50
  127.4 211.7 %all-reduce.30.cloned.1.call-start = ((), (), s32[]{:S(2)}) async-start(), calls=%async_computation.12 | async-start | bytes 8388608 | tf_op jit(solution)/shard_map/psum | solution.py:45
  253.2 85.9 %copy-start.93 = (f32[512]{0:T(512)S(1)}, f32[512]{0:T(512)}, u32[]{:S(2)}) copy-start(f32[512]{0:T(512)} %param.50) | copy-start | bytes 6148
  253.2 164.1 %all-reduce.32.cloned.1.call-start = ((), (), s32[]{:S(2)}) async-start(), calls=%async_computation.13 | async-start | bytes 4194304 | tf_op jit(solution)/shard_map/psum | solution.py:57
  343.4 83.0 %copy-start.46 = (f32[8,256]{1,0:T(8,128)}, f32[8,256]{1,0:T(8,128)S(1)}, u32[]{:S(2)}) copy-start(f32[8,256]{1,0:T(8,128)S(1)} %broadcast_multiply_fusion.1) | copy-start | bytes 24580
  365.6 159.1 %all-reduce.34.cloned.1.call-start = ((), (), s32[]{:S(2)}) async-start(), calls=%async_computation.14 | async-start | bytes 8388608 | tf_op jit(solution)/shard_map/psum | solution.py:63
  439.0 151.5 %all-reduce.36.cloned.1.call-start = ((), (), s32[]{:S(2)}) async-start(), calls=%async_computation.15 | async-start | bytes 1572864 | tf_op jit(solution)/shard_map/psum | solution.py:56
  555.6 114.2 %reduce-scatter.34.cloned.1.call-start = ((), (), s32[]{:S(2)}) async-start(), calls=%async_computation.24 | async-start | bytes 294912
  561.8 158.4 %reduce-scatter.32.cloned.1.call-start = ((), (), s32[]{:S(2)}) async-start(), calls=%async_computation.23 | async-start | bytes 589824
  571.1 213.7 %reduce-scatter.30.cloned.1.call-start = ((), (), s32[]{:S(2)}) async-start(), calls=%async_computation.22 | async-start | bytes 884736
  608.6 242.2 %all-reduce.38.cloned.1.call-start = ((), (), s32[]{:S(2)}) async-start(), calls=%async_computation.25 | async-start | bytes 5767168 | tf_op jit(solution)/shard_map/psum | solution.py:51
  630.3 376.8 %reduce-scatter.28.cloned.1.call-start = ((), (), s32[]{:S(2)}) async-start(), calls=%async_computation.21 | async-start | bytes 2211840
  643.3 365.9 %reduce-scatter.24.cloned.1.call-start = ((), (), s32[]{:S(2)}) async-start(), calls=%async_computation.19 | async-start | bytes 1179648 | tf_op jit(solution)/shard_map/reduce_scatter | solution.py:347
  649.2 405.5 %reduce-scatter.26.cloned.1.call-start = ((), (), s32[]{:S(2)}) async-start(), calls=%async_computation.20 | async-start | bytes 1179648 | tf_op jit(solution)/shard_map/reduce_scatter | solution.py:349
  653.8 468.7 %reduce-scatter.22.cloned.1.call-start = ((), (), s32[]{:S(2)}) async-start(), calls=%async_computation.18 | async-start | bytes 1769472 | tf_op jit(solution)/shard_map/reduce_scatter | solution.py:351
  657.2 537.3 %reduce-scatter.18.cloned.1.call-start = ((), (), s32[]{:S(2)}) async-start(), calls=%async_computation.16 | async-start | bytes 2654208 | tf_op jit(solution)/shard_map/reduce_scatter | solution.py:336
  661.2 605.8 %reduce-scatter.20.cloned.1.call-start = ((), (), s32[]{:S(2)}) async-start(), calls=%async_computation.17 | async-start | bytes 2654208 | tf_op jit(solution)/shard_map/reduce_scatter | solution.py:338
  666.1 184.7 %copy-start.58 = (f32[8,64]{1,0:T(8,128)S(1)}, f32[8,64]{1,0:T(8,128)}, u32[]{:S(2)}) copy-start(f32[8,64]{1,0:T(8,128)} %copy-done.56) | copy-start | bytes 6148
  666.1 184.7 %copy-start.72 = (f32[768]{0:T(1024)S(1)}, f32[768]{0:T(1024)}, u32[]{:S(2)}) copy-start(f32[768]{0:T(1024)} %param.32) | copy-start | bytes 9220
  786.4 130.9 %copy-start.15 = (f32[8,64,768]{2,1,0:T(8,128)S(1)}, f32[8,64,768]{2,1,0:T(8,128)}, u32[]{:S(2)}) copy-start(f32[8,64,768]{2,1,0:T(8,128)} %copy-done.14) | copy-start | bytes 4718596
  (99 other events, 603.3 us)
Sparse Core Ops, SparseCore 0:
  20.7 31.2 all-gather.1
  70.0 42.8 all-reduce.25
  127.5 42.8 all-reduce.27
  253.4 85.7 all-reduce.29
  365.7 51.5 all-reduce.31
  439.1 85.5 all-reduce.33
  555.7 34.7 all-reduce.35
  594.2 61.2 reduce-scatter.33
  659.2 60.9 reduce-scatter.31
  723.3 61.4 reduce-scatter.29
  787.5 63.2 all-reduce.37
  854.5 66.9 reduce-scatter.27
  925.5 62.3 reduce-scatter.23
  992.2 62.4 reduce-scatter.25
  1058.6 63.8 reduce-scatter.21
  1126.8 67.6 reduce-scatter.17
  1198.9 68.1 reduce-scatter.19
where the time goes:
time: 1290 us; the launch traced here: 1270 us
  waiting for transfers between devices  744 us (58%)
  local copies, waits for them, and re-layouts  279 us (22%)
  matrix products  101 us (8%)
  other arithmetic  92.6 us (7%)
  blocking collectives  39.1 us (3%)
  between operations  16.8 us (1%)
    psum x2, waiting for transfers between devices, attn_sum(): return lax.psum(partial_out, 'tensor')  127 us
    unnamed x21, waiting for transfers between devices  111 us
    reduce_scatter x1, waiting for transfers between devices, body(): lax.psum_scatter(enc_grads[9], 'dp', scatter_dimension=1, tiled=True)  72.5 us
    reduce_scatter x1, waiting for transfers between devices, body(): lax.psum_scatter(enc_grads[7], 'dp', scatter_dimension=0, tiled=True)  72 us
    psum x2, waiting for transfers between devices, mlp_back_sum(): lax.psum(partial_grad.astype(jnp.bfloat16), 'tensor').astype(jnp.float32)  70.3 us
    scatter x1, local copies, waits for them, and re-layouts, body(): grad_mean = jnp.zeros((chip_count, patches, enc_width), jnp.float32).at[c...  69.8 us
    reduce_scatter x1, waiting for transfers between devices, body(): lax.psum_scatter(grad_proj_weight, 'dp', scatter_dimension=0, tiled=True)  67.8 us
    scatter x1, local copies, waits for them, and re-layouts, body(): jnp.broadcast_to(mask_token, cotangent.shape).at[chip_rows, visible_index]  64.5 us
  transfers between devices with their start and end apart: 17, of which 14 were waited for; matrix products, arithmetic and copies ran while one was open for 20% of the time, Pallas kernels for 0%

commit v1 on v0

v1 whole, which is shorter than its diff:
```python
import functools
import math

import jax
import jax.numpy as jnp
from jax import lax
from jax.experimental import pallas as pl
from jax.experimental.pallas import tpu as pltpu
from jax.sharding import PartitionSpec as P

HEAD = 64
EPSILON = 1e-05
SCALE = HEAD ** (-0.5)
VMEM_BYTES = 52 * 1024 * 1024
F32 = jnp.float32
LOW = jnp.bfloat16
NN = (((1,), (0,)), ((), ()))
NT = (((1,), (1,)), ((), ()))
TN = (((0,), (0,)), ((), ()))
VEC_ROWS = 16


def dot(left, right, dims=NN):
    return lax.dot_general(left, right, dims, preferred_element_type=F32)


def col_sum(values):
    return jnp.sum(values, 0, keepdims=True)


def norm_parts(stream):
    center = stream - jnp.mean(stream, -1, keepdims=True)
    inverse = lax.rsqrt(jnp.mean(center * center, -1, keepdims=True) + EPSILON)
    return center * inverse, inverse


def norm_back(grad, xhat, inverse, gain):
    scaled = grad * gain
    mean_q = jnp.mean(scaled, -1, keepdims=True)
    mean_qx = jnp.mean(scaled * xhat, -1, keepdims=True)
    return inverse * (scaled - mean_q - xhat * mean_qx)


def gelu_parts(hidden):
    phi = 0.5 + 0.5 * lax.erf(hidden * (0.5**0.5))
    density = jnp.exp(hidden * hidden * -0.5) * (1.0 / math.sqrt(2.0 * math.pi))
    return hidden * phi, phi + hidden * density


def softmax_rows(scores):
    weights = jnp.exp(scores - jnp.max(scores, -1, keepdims=True))
    return weights * (1.0 / jnp.sum(weights, -1, keepdims=True))


def same_chip(rows, length):
    first = lax.broadcasted_iota(jnp.int32, (rows, rows), 0) // length
    second = lax.broadcasted_iota(jnp.int32, (rows, rows), 1) // length
    return first == second


def attend(queries, keyset, mask):
    scores = dot(queries, keyset, NT) * SCALE
    if mask is not None:
        scores = jnp.where(mask, scores, -1e30)
    return softmax_rows(scores)


def attend_back(probs, queries, keyset, valset, grad_mixed):
    grad_probs = dot(grad_mixed, valset, NT)
    grad_values = dot(probs.astype(LOW), grad_mixed, TN)
    grad_scores = probs * (grad_probs - jnp.sum(grad_probs * probs, -1, keepdims=True))
    score_low = grad_scores.astype(LOW)
    grad_queries = dot(score_low, keyset) * SCALE
    grad_keys = dot(score_low, queries, TN) * SCALE
    return grad_queries.astype(LOW), grad_keys.astype(LOW), grad_values.astype(LOW)


def call(body, out_shape, args, scalars=(), flops=0, name=None):
    specs = [pl.BlockSpec(memory_space=pltpu.SMEM) for _ in scalars]
    specs += [pl.BlockSpec(memory_space=pltpu.VMEM) for _ in args]
    moved = sum(math.prod(a.shape) * a.dtype.itemsize for a in list(args) + list(out_shape))
    return pl.pallas_call(
        body,
        out_shape=out_shape,
        in_specs=specs,
        out_specs=[pl.BlockSpec(memory_space=pltpu.VMEM) for _ in out_shape],
        compiler_params=pltpu.CompilerParams(vmem_limit_bytes=VMEM_BYTES),
        cost_estimate=pl.CostEstimate(flops=flops, bytes_accessed=moved, transcendentals=0),
        name=name,
    )(*scalars, *args)


def bit_reverse(value, bits):
    result = 0
    for place in range(bits):
        result = result | (((value >> place) & 1) << (bits - 1 - place))
    return result


def put_block(keep, send, lead, place, half, rows, columns, values):
    @pl.when(place < half)
    def _():
        keep[lead + (place, rows, columns)] = values

    @pl.when(place >= half)
    def _():
        send[lead + (place - half, rows, columns)] = values


def band_mean_kernel(place_ref, count_ref, bands_ref, visible_ref, out_ref, *, own_chips):
    spot, rank = chip_of(pl.program_id(0), place_ref[0], own_chips), place_ref[0]
    count = count_ref[spot]
    own = bands_ref.shape[2]
    total = bands_ref[0, 0].astype(F32)
    for band in range(1, bands_ref.shape[1]):
        used = jnp.where(band < count, 1.0, 0.0).astype(F32)
        total = total + bands_ref[0, band].astype(F32) * used
    mean = (total / count.astype(F32)).astype(LOW)
    patch = lax.broadcasted_iota(jnp.int32, (visible_ref.shape[1], own), 1) + rank * own
    chosen = jnp.where(visible_ref[0] == patch, 1.0, 0.0).astype(LOW)
    out_ref[0] = dot(chosen, mean).astype(LOW)


def chip_of(step, rank, own_chips):
    part, index = step // own_chips, step % own_chips
    apart = 2 * (part % 2) + part // 2
    return (rank ^ apart) * own_chips + index


def band_mean(place, counts, bands, visible, own_chips):
    chips, band_count, own, width = bands.shape
    length = visible.shape[1]
    grid_spec = pltpu.PrefetchScalarGridSpec(
        num_scalar_prefetch=2,
        grid=(chips,),
        in_specs=[
            pl.BlockSpec(
                (1, band_count, own, width), lambda g, p, c: (chip_of(g, p[0], own_chips), 0, 0, 0)
            ),
            pl.BlockSpec((1, length, 1), lambda g, p, c: (chip_of(g, p[0], own_chips), 0, 0)),
        ],
        out_specs=pl.BlockSpec((1, length, width), lambda g, p, c: (g, 0, 0)),
    )
    return pl.pallas_call(
        functools.partial(band_mean_kernel, own_chips=own_chips),
        grid_spec=grid_spec,
        out_shape=jax.ShapeDtypeStruct((chips, length, width), LOW),
        compiler_params=pltpu.CompilerParams(vmem_limit_bytes=VMEM_BYTES),
        cost_estimate=pl.CostEstimate(
            flops=bands.size, bytes_accessed=2 * bands.size, transcendentals=0
        ),
        name="band_mean",
    )(place, counts, bands, visible[:, :, None])


def enc_attn_kernel(
    tok_a, tok_b, gain, shift, qkv_w, out_w, part_a, part_b, normed_ref, qkv_ref, mixed_ref, *, length
):
    rows = tok_a.shape[0]
    inner = out_w.shape[0]
    mask = same_chip(rows, length)
    for group, (tok, part) in enumerate(((tok_a, part_a), (tok_b, part_b))):
        span = slice(group * rows, (group + 1) * rows)
        xhat, _ = norm_parts(tok[...].astype(F32))
        normed = (xhat * gain[...] + shift[...]).astype(LOW)
        normed_ref[span] = normed
        qkv = dot(normed, qkv_w[...], NT).astype(LOW)
        qkv_ref[span] = qkv
        heads = []
        for head in range(inner // HEAD):
            at = [qkv[:, k * inner + head * HEAD : k * inner + (head + 1) * HEAD] for k in range(3)]
            probs = attend(at[0], at[1], mask)
            heads.append(dot(probs.astype(LOW), at[2]).astype(LOW))
        mixed = jnp.concatenate(heads, 1)
        mixed_ref[span] = mixed
        part[...] = dot(mixed, out_w[...]).astype(LOW)


def enc_mlp_kernel(
    tok_a, tok_b, sum_a, sum_b, out_bias, gain, shift, up_w, up_bias, down_w,
    part_a, part_b, normed_ref, act_ref, slope_ref,
):
    rows = tok_a.shape[0]
    groups = ((tok_a, sum_a, part_a), (tok_b, sum_b, part_b))
    for group, (tok, total, part) in enumerate(groups):
        span = slice(group * rows, (group + 1) * rows)
        middle = tok[...].astype(F32) + total[...].astype(F32) + out_bias[...]
        xhat, _ = norm_parts(middle)
        normed = (xhat * gain[...] + shift[...]).astype(LOW)
        normed_ref[span] = normed
        activation, slope = gelu_parts(dot(normed, up_w[...]) + up_bias[...])
        act_low = activation.astype(LOW)
        act_ref[span] = act_low
        slope_ref[span] = slope.astype(LOW)
        part[...] = dot(act_low, down_w[...]).astype(LOW)


def enc_mlp_back_kernel(
    lat_a, lat_b, proj_w, slope_ref, up_w, down_w,
    part_a, part_b, out_a, out_b, low_ref, hidden_ref, vec_ref,
):
    rows = lat_a.shape[0]
    down_sum, up_sum = 0.0, 0.0
    groups = ((lat_a, out_a, part_a), (lat_b, out_b, part_b))
    for group, (lat, out, part) in enumerate(groups):
        span = slice(group * rows, (group + 1) * rows)
        grad_out = dot(lat[...], proj_w[...], NT)
        out[...] = grad_out
        grad_low = grad_out.astype(LOW)
        low_ref[span] = grad_low
        grad_hidden = dot(grad_low, down_w[...], NT) * slope_ref[span].astype(F32)
        hidden_low = grad_hidden.astype(LOW)
        hidden_ref[span] = hidden_low
        down_sum = down_sum + col_sum(grad_out)
        up_sum = up_sum + col_sum(grad_hidden)
        part[...] = dot(hidden_low, up_w[...], NT).astype(LOW)
    vec_ref[...] = jnp.concatenate(
        [down_sum, up_sum, jnp.zeros((vec_ref.shape[0] - 2, down_sum.shape[1]), F32)], 0
    )


def enc_mlp_weights_kernel(
    place_ref, normed_ref, hidden_ref, low_ref, act_ref, lat_a, lat_b, enc_a, enc_b, keep, send
):
    half = keep.shape[0]
    blocks, bits = 2 * half, (2 * half).bit_length() - 1
    width, hidden = normed_ref.shape[1], hidden_ref.shape[1]
    proj_own = keep.shape[2] - 2 * hidden
    own = pl.ds(pl.multiple_of(place_ref[0] * proj_own, proj_own), proj_own)
    up = dot(normed_ref[...], hidden_ref[...], TN).astype(LOW)
    down = dot(low_ref[...], act_ref[...], TN).astype(LOW)
    proj = (dot(enc_a[...], lat_a[:, own], TN) + dot(enc_b[...], lat_b[:, own], TN)).astype(LOW)
    piece = width // blocks
    for block in range(blocks):
        at = slice(block * piece, (block + 1) * piece)
        values = jnp.concatenate([up[at], down[at], proj[at]], 1)
        place = place_ref[1] ^ bit_reverse(block, bits)
        put_block(keep, send, (), place, half, slice(0, piece), slice(None), values)


def enc_attn_back_kernel(
    tok_a, tok_b, sum_a, sum_b, out_bias, mlp_gain, out_a, out_b, back_a, back_b,
    qkv_ref, qkv_w, out_w, part_a, part_b, mid_a, mid_b, low_ref, grad_qkv_ref, vec_ref, *, length
):
    rows = tok_a.shape[0]
    inner = out_w.shape[0]
    mask = same_chip(rows, length)
    sums = [0.0] * 5
    groups = (
        (tok_a, sum_a, out_a, back_a, part_a, mid_a),
        (tok_b, sum_b, out_b, back_b, part_b, mid_b),
    )
    for group, (tok, total, out, back, part, mid) in enumerate(groups):
        span = slice(group * rows, (group + 1) * rows)
        stream = tok[...].astype(F32)
        xhat, inverse = norm_parts(stream + total[...].astype(F32) + out_bias[...])
        grad = back[...].astype(F32)
        sums[0] = sums[0] + col_sum(grad * xhat)
        sums[1] = sums[1] + col_sum(grad)
        grad_middle = out[...] + norm_back(grad, xhat, inverse, mlp_gain[...])
        mid[...] = grad_middle
        sums[2] = sums[2] + col_sum(grad_middle)
        middle_low = grad_middle.astype(LOW)
        low_ref[span] = middle_low
        grad_mixed = dot(middle_low, out_w[...], NT).astype(LOW)
        grads = ([], [], [])
        for head in range(inner // HEAD):
            at = [
                qkv_ref[span, k * inner + head * HEAD : k * inner + (head + 1) * HEAD]
                for k in range(3)
            ]
            probs = attend(at[0], at[1], mask)
            found = attend_back(probs, *at, grad_mixed[:, head * HEAD : (head + 1) * HEAD])
            for kind in range(3):
                grads[kind].append(found[kind])
        grad_qkv = jnp.concatenate(grads[0] + grads[1] + grads[2], 1)
        grad_qkv_ref[span] = grad_qkv
        partial = dot(grad_qkv, qkv_w[...])
        part[...] = partial.astype(LOW)
        xhat, _ = norm_parts(stream)
        sums[3] = sums[3] + col_sum(partial * xhat)
        sums[4] = sums[4] + col_sum(partial)
    vec_ref[...] = jnp.concatenate(
        sums + [jnp.zeros((vec_ref.shape[0] - 5, sums[0].shape[1]), F32)], 0
    )


def enc_attn_weights_kernel(
    place_ref, normed_ref, grad_qkv_ref, low_ref, mixed_ref, vec_mlp, vec_attn, keep, send
):
    half = keep.shape[0]
    blocks, bits = 2 * half, (2 * half).bit_length() - 1
    width = normed_ref.shape[1]
    qkv = dot(normed_ref[...], grad_qkv_ref[...], TN).astype(LOW)
    out = dot(low_ref[...], mixed_ref[...], TN).astype(LOW)
    vectors = jnp.concatenate([vec_mlp[...], vec_attn[...]], 0)
    piece = width // blocks
    first = keep.shape[1] - VEC_ROWS
    for block in range(blocks):
        at = slice(block * piece, (block + 1) * piece)
        place = place_ref[1] ^ bit_reverse(block, bits)
        values = jnp.concatenate([qkv[at], out[at]], 1)
        put_block(keep, send, (), place, half, slice(0, piece), slice(None), values)
        put_block(
            keep, send, (), place, half, slice(first, first + VEC_ROWS), slice(0, piece),
            vectors[:, at].astype(LOW),
        )


def band_grad_kernel(
    place_ref, count_ref, tok_ref, back_ref, mid_ref, gain, visible_ref, out_ref, *, own_chips
):
    rank = place_ref[0]
    count = count_ref[chip_of(pl.program_id(0), rank, own_chips)]
    xhat, inverse = norm_parts(tok_ref[0].astype(F32))
    grad = mid_ref[0] + norm_back(back_ref[0].astype(F32), xhat, inverse, gain[...])
    grad = grad / count.astype(F32)
    own, length = out_ref.shape[2], visible_ref.shape[2]
    patch = lax.broadcasted_iota(jnp.int32, (own, length), 0) + rank * own
    chosen = jnp.where(visible_ref[0] == patch, 1.0, 0.0).astype(LOW)
    high = grad.astype(LOW)
    rest = (grad - high.astype(F32)).astype(LOW)
    spread = dot(chosen, high) + dot(chosen, rest)
    for band in range(out_ref.shape[1]):
        used = jnp.where(band < count, 1.0, 0.0).astype(F32)
        out_ref[0, band] = spread * used


def band_grad_call(place, counts, tokens, back, mid, gain, visible, bands, own_chips):
    chips, band_count, own, width = bands
    length = visible.shape[1]
    by_step = pl.BlockSpec((1, length, width), lambda g, p, c: (g, 0, 0))
    grid_spec = pltpu.PrefetchScalarGridSpec(
        num_scalar_prefetch=2,
        grid=(chips,),
        in_specs=[
            by_step,
            by_step,
            by_step,
            pl.BlockSpec((1, width), lambda g, p, c: (0, 0)),
            pl.BlockSpec((1, 1, length), lambda g, p, c: (chip_of(g, p[0], own_chips), 0, 0)),
        ],
        out_specs=pl.BlockSpec(
            (1, band_count, own, width), lambda g, p, c: (chip_of(g, p[0], own_chips), 0, 0, 0)
        ),
    )
    return pl.pallas_call(
        functools.partial(band_grad_kernel, own_chips=own_chips),
        grid_spec=grid_spec,
        out_shape=jax.ShapeDtypeStruct(bands, F32),
        compiler_params=pltpu.CompilerParams(vmem_limit_bytes=VMEM_BYTES),
        cost_estimate=pl.CostEstimate(
            flops=0, bytes_accessed=4 * math.prod(bands), transcendentals=0
        ),
        name="band_grad",
    )(place, counts, tokens, back, mid, gain, visible[:, None, :])


def dec_kernel(
    place_ref, enc_low, proj_w, proj_bias, mask_token, position, visible_col, visible_row,
    attn_gain, attn_shift, out_bias, mlp_gain, mlp_shift, up_bias, down_bias,
    w0, w1, w2, w3, cotangent,
    decoded_keep, decoded_send, grad_latent_ref, n1_ref, n2_ref, gml_ref, act_ref, hid_ref,
    gqkv_ref, mixed_ref, vec_ref, upvec_ref,
    slope_scr, prob_scr,
):
    weights = (w0, w1, w2, w3)
    patches, width = position.shape
    kinds = 3 * HEAD
    inner = kinds + HEAD
    units = up_bias.shape[2]
    up_at, down_at = slice(inner, inner + width), slice(inner + width, inner + width + units)
    step = pl.program_id(0)
    latent = dot(enc_low[0], proj_w[...]) + proj_bias[...]
    length = latent.shape[0]
    hit = lax.broadcasted_iota(jnp.int32, (patches, length), 0) == visible_row[0]
    chosen = jnp.where(hit, 1.0, 0.0).astype(LOW)
    is_visible = jnp.sum(jnp.where(hit, 1.0, 0.0), 1, keepdims=True)
    high = latent.astype(LOW)
    rest = (latent - high.astype(F32)).astype(LOW)
    stream = dot(chosen, high) + dot(chosen, rest)
    stream = stream + (1.0 - is_visible) * mask_token[...] + position[...]
    xhat1, inverse1 = norm_parts(stream)
    n1 = (xhat1 * attn_gain[...] + attn_shift[...]).astype(LOW)
    n1_ref[...] = n1
    qkvs, mixed = [], []
    for part, weight in enumerate(weights):
        qkv = dot(n1, weight[0:kinds], NT).astype(LOW)
        at = [qkv[:, k * HEAD : (k + 1) * HEAD] for k in range(3)]
        probs = attend(at[0], at[1], None)
        prob_scr[part] = probs
        mixed_one = dot(probs.astype(LOW), at[2]).astype(LOW)
        mixed_ref[part] = mixed_one
        qkvs.append(at)
        mixed.append(mixed_one)
    out_all = jnp.concatenate([weight[kinds:inner] for weight in weights], 0)
    middle = stream + dot(jnp.concatenate(mixed, 1), out_all) + out_bias[...]
    xhat2, inverse2 = norm_parts(middle)
    n2 = (xhat2 * mlp_gain[...] + mlp_shift[...]).astype(LOW)
    n2_ref[...] = n2
    total = middle + down_bias[...]
    for part, weight in enumerate(weights):
        activation, slope = gelu_parts(dot(n2, weight[up_at]) + up_bias[part])
        act_low = activation.astype(LOW)
        act_ref[part] = act_low
        slope_scr[part] = slope.astype(LOW)
        total = total + dot(act_low, weight[down_at])
    parts = len(weights)
    column = width // parts
    for part in range(parts):
        values = total[:, part * column : (part + 1) * column].astype(LOW)
        apart = place_ref[0] ^ part

        @pl.when(apart % 2 == 0)
        def _(values=values, apart=apart):
            decoded_keep[apart // 2, 0] = values

        @pl.when(apart % 2 == 1)
        def _(values=values, apart=apart):
            decoded_send[apart // 2, 0] = values

    grad_low = cotangent[0]
    grad_out = grad_low.astype(F32)
    grad_n2 = 0.0
    up_sums = []
    for part, weight in enumerate(weights):
        grad_hidden = dot(grad_low, weight[down_at], NT) * slope_scr[part].astype(F32)
        hidden_low = grad_hidden.astype(LOW)
        hid_ref[part] = hidden_low
        up_sums.append(col_sum(grad_hidden))
        grad_n2 = grad_n2 + dot(hidden_low, weight[up_at], NT)
    grad_middle = grad_out + norm_back(grad_n2, xhat2, inverse2, mlp_gain[...])
    mlp_gain_sum, mlp_shift_sum = col_sum(grad_n2 * xhat2), col_sum(grad_n2)
    middle_low = grad_middle.astype(LOW)
    gml_ref[...] = middle_low
    grad_mixed = dot(middle_low, out_all, NT).astype(LOW)
    grad_n1 = 0.0
    for part, weight in enumerate(weights):
        own = grad_mixed[:, part * HEAD : (part + 1) * HEAD]
        grad_qkv = jnp.concatenate(attend_back(prob_scr[part], *qkvs[part], own), 1)
        gqkv_ref[part] = grad_qkv
        grad_n1 = grad_n1 + dot(grad_qkv, weight[0:kinds])
    grad_stream = grad_middle + norm_back(grad_n1, xhat1, inverse1, attn_gain[...])
    pick = lax.broadcasted_iota(jnp.int32, (length, patches), 1) == visible_col[0]
    grad_latent_ref[0] = dot(
        jnp.where(pick, 1.0, 0.0).astype(LOW), grad_stream.astype(LOW)
    ).astype(LOW)
    seen_sum = col_sum(grad_stream * is_visible)
    vectors = jnp.concatenate(
        [
            col_sum(grad_n1 * xhat1),
            col_sum(grad_n1),
            col_sum(grad_middle),
            mlp_gain_sum,
            mlp_shift_sum,
            col_sum(grad_out),
            seen_sum,
            col_sum(grad_stream) - seen_sum,
        ],
        0,
    )
    ups = jnp.concatenate(up_sums + [jnp.zeros((4, units), F32)], 0)

    @pl.when(step == 0)
    def _():
        vec_ref[...] = vectors
        upvec_ref[...] = ups

    @pl.when(step > 0)
    def _():
        vec_ref[...] += vectors
        upvec_ref[...] += ups


def dec_call(place, enc_low, small, position, visible, up_bias, weights, cotangent):
    chips, length, enc_width = enc_low.shape
    patches, width = position.shape
    parts, units = up_bias.shape[0], up_bias.shape[2]
    rows = chips * patches
    column = width // parts
    proj_w, proj_bias, mask_token, rest = small

    def whole(array):
        dims = array.ndim
        return pl.BlockSpec(array.shape, lambda i, p: (0,) * dims)

    def by_chip(shape):
        return pl.BlockSpec((1,) + shape[1:], lambda i, p: (i, 0, 0))

    def by_rows(columns):
        return pl.BlockSpec((patches, columns), lambda i, p: (i, 0))

    def by_part(columns):
        return pl.BlockSpec((parts, patches, columns), lambda i, p: (0, i, 0))

    visible_col, visible_row = visible[:, :, None], visible[:, None, :]
    whole_args = [proj_w, proj_bias, mask_token, position]
    args = [enc_low, *whole_args, visible_col, visible_row, *rest[:5], up_bias, rest[5], *weights]
    specs = [by_chip(enc_low.shape)] + [whole(a) for a in whole_args]
    specs += [by_chip(visible_col.shape), by_chip(visible_row.shape)]
    specs += [whole(a) for a in args[7:]]
    args.append(cotangent)
    specs.append(by_chip(cotangent.shape))
    half = parts // 2
    decoded_spec = pl.BlockSpec((half, 1, patches, column), lambda i, p: (0, i, 0, 0))
    shape = jax.ShapeDtypeStruct
    out_shape = [
        shape((half, chips, patches, column), LOW),
        shape((half, chips, patches, column), LOW),
        shape((chips, length, width), LOW),
        shape((rows, width), LOW),
        shape((rows, width), LOW),
        shape((rows, width), LOW),
        shape((parts, rows, units), LOW),
        shape((parts, rows, units), LOW),
        shape((parts, rows, 3 * HEAD), LOW),
        shape((parts, rows, HEAD), LOW),
        shape((8, width), F32),
        shape((8, units), F32),
    ]
    out_specs = [
        decoded_spec,
        decoded_spec,
        pl.BlockSpec((1, length, width), lambda i, p: (i, 0, 0)),
        by_rows(width),
        by_rows(width),
        by_rows(width),
        by_part(units),
        by_part(units),
        by_part(3 * HEAD),
        by_part(HEAD),
        pl.BlockSpec((8, width), lambda i, p: (0, 0)),
        pl.BlockSpec((8, units), lambda i, p: (0, 0)),
    ]
    return pl.pallas_call(
        dec_kernel,
        grid_spec=pltpu.PrefetchScalarGridSpec(
            num_scalar_prefetch=1,
            grid=(chips,),
            in_specs=specs,
            out_specs=out_specs,
            scratch_shapes=[
                pltpu.VMEM((parts, patches, units), LOW),
                pltpu.VMEM((parts, patches, patches), F32),
            ],
        ),
        out_shape=out_shape,
        compiler_params=pltpu.CompilerParams(vmem_limit_bytes=VMEM_BYTES),
        cost_estimate=pl.CostEstimate(
            flops=12 * rows * width * units * parts // 2, bytes_accessed=1 << 24, transcendentals=0
        ),
        name="decoder",
    )(place, *args)


def dec_weights_kernel(
    place_ref, n1_ref, n2_ref, gml_ref, cot_ref, act_ref, hid_ref, gqkv_ref, mixed_ref,
    vec_ref, upvec_ref, out_ref, *, first
):
    blocks = out_ref.shape[1]
    bits = blocks.bit_length() - 1
    width = n1_ref.shape[1]
    up = dot(n2_ref[...], hid_ref[0], TN).astype(LOW)
    down = dot(cot_ref[...], act_ref[0], TN).astype(LOW)
    qkv = dot(n1_ref[...], gqkv_ref[0], TN).astype(LOW)
    out = dot(gml_ref[...], mixed_ref[0], TN).astype(LOW)
    which = first + 2 * pl.program_id(0)
    vectors = jnp.concatenate(
        [
            vec_ref[...],
            upvec_ref[pl.ds(which, 1)],
            jnp.zeros((VEC_ROWS - 9, width), F32),
        ],
        0,
    ).astype(LOW)
    piece = width // blocks
    start = out_ref.shape[2] - VEC_ROWS
    for block in range(blocks):
        at = slice(block * piece, (block + 1) * piece)
        place = place_ref[1] ^ bit_reverse(block, bits)
        values = jnp.concatenate([up[at], down[at], qkv[at], out[at]], 1)
        out_ref[0, place, 0:piece] = values
        out_ref[0, place, start : start + VEC_ROWS, 0:piece] = vectors[:, at]


def dec_weights(place, saved, vectors, blocks, first):
    n1, n2, gml, cot, act, hid, gqkv, mixed = saved
    rows, width = n1.shape
    units = act.shape[2]
    piece = width // blocks
    padded = -(-piece // 16) * 16 + VEC_ROWS
    columns = 2 * units + 4 * HEAD

    def whole(array):
        dims = array.ndim
        return pl.BlockSpec(array.shape, lambda g, p: (0,) * dims)

    def by_part(array):
        return pl.BlockSpec((1,) + array.shape[1:], lambda g, p: (first + 2 * g, 0, 0))

    return pl.pallas_call(
        functools.partial(dec_weights_kernel, first=first),
        grid_spec=pltpu.PrefetchScalarGridSpec(
            num_scalar_prefetch=1,
            grid=(2,),
            in_specs=[whole(a) for a in (n1, n2, gml, cot)]
            + [by_part(a) for a in (act, hid, gqkv, mixed)]
            + [whole(a) for a in vectors],
            out_specs=pl.BlockSpec(
                (1, blocks, padded, columns), lambda g, p: (g, 0, 0, 0)
            ),
        ),
        out_shape=jax.ShapeDtypeStruct((2, blocks, padded, columns), LOW),
        compiler_params=pltpu.CompilerParams(vmem_limit_bytes=VMEM_BYTES),
        cost_estimate=pl.CostEstimate(
            flops=4 * rows * width * columns, bytes_accessed=1 << 23, transcendentals=0
        ),
        name="dec_weights_%d" % first,
    )(place, n1, n2, gml, cot, act, hid, gqkv, mixed, *vectors)


def swap(values, axis, apart):
    size = lax.axis_size(axis)
    return lax.ppermute(values, axis, [(i, i ^ apart) for i in range(size)])


def add_low(first, second):
    return (first.astype(F32) + second.astype(F32)).astype(LOW)


def sum_over_tensor(keep, send):
    rows = keep.shape[0]
    own = add_low(keep, swap(send, "tensor", 1))
    other = swap(own, "tensor", 2).reshape(2, rows // 2, -1)
    total = add_low(own.reshape(2, rows // 2, -1), other[::-1]).reshape(keep.shape)
    return total, swap(total, "tensor", 1)


def dp_steps(keep, send, axis="dp"):
    distance = 1
    while True:
        total = keep.astype(F32) + swap(send, axis, distance).astype(F32)
        if total.shape[0] == 1:
            return total[0]
        distance *= 2
        half = total.shape[0] // 2
        keep, send = total[:half], total[half:].astype(LOW)


def gather_low(own):
    first = jnp.concatenate([own, swap(own, "tensor", 2)], 0)
    return first, swap(first, "tensor", 1)


def to_absolute(values, rank):
    values = jnp.where(rank // 2 == 1, values[::-1], values)
    return jnp.where(rank % 2 == 1, values[:, ::-1], values)


def body(
    band_patches,
    band_counts,
    visible_index,
    enc_attn_gain,
    enc_attn_shift,
    enc_qkv_weight,
    enc_out_weight,
    enc_out_bias,
    enc_mlp_gain,
    enc_mlp_shift,
    enc_up_weight,
    enc_up_bias,
    enc_down_weight,
    enc_down_bias,
    proj_weight,
    proj_bias,
    mask_token,
    dec_attn_gain,
    dec_attn_shift,
    dec_qkv_weight,
    dec_out_weight,
    dec_out_bias,
    dec_mlp_gain,
    dec_mlp_shift,
    dec_up_weight,
    dec_up_bias,
    dec_down_weight,
    dec_down_bias,
    cotangent,
):
    parts = lax.axis_size("tensor")
    blocks = lax.axis_size("dp")
    bits = blocks.bit_length() - 1
    rank = lax.axis_index("tensor")
    place = jnp.stack([rank, bit_reverse(lax.axis_index("dp"), bits)]).astype(jnp.int32)
    chips, length = visible_index.shape
    own_chips = chips // parts
    enc_width = band_patches.shape[3]
    patches, dec_width = cotangent.shape[1:]
    enc_inner = enc_out_weight.shape[0]
    enc_units = enc_up_weight.shape[1]
    dec_units = dec_up_weight.shape[1]
    dec_kinds = 3 * dec_out_weight.shape[0]
    rows = chips * length
    shape = jax.ShapeDtypeStruct

    def row(vector):
        return vector.reshape(1, -1)

    w_own = jnp.concatenate(
        [
            dec_qkv_weight.reshape(dec_kinds, dec_width),
            dec_out_weight,
            dec_up_weight,
            dec_down_weight,
        ],
        0,
    )
    w_core = swap(w_own, "tensor", 1)
    w_x = swap(w_own, "tensor", 2)
    w_diag = swap(w_x, "tensor", 1)
    weights = (w_own, w_core, w_x, w_diag)
    up_bias_parts = to_absolute(dec_up_bias.reshape(2, 2, 1, dec_units), rank)
    up_bias_parts = up_bias_parts.reshape(parts, 1, dec_units)

    tokens_part = band_mean(place, band_counts, band_patches, visible_index, own_chips)
    tokens_part = tokens_part.reshape(2, rows // 2, enc_width)
    tok_a, tok_b = sum_over_tensor(tokens_part[0], tokens_part[1])

    half_rows = shape((rows // 2, enc_width), LOW)
    all_rows = shape((rows, enc_width), LOW)
    qkv_w = enc_qkv_weight.reshape(3 * enc_inner, enc_width)
    flops_attn = 2 * rows * enc_width * 4 * enc_inner
    flops_mlp = 4 * rows * enc_width * enc_units
    part_a, part_b, enc_n1, enc_qkv, enc_mixed = call(
        functools.partial(enc_attn_kernel, length=length),
        [half_rows, half_rows, all_rows, shape((rows, 3 * enc_inner), LOW), shape((rows, enc_inner), LOW)],
        [tok_a, tok_b, row(enc_attn_gain), row(enc_attn_shift), qkv_w, enc_out_weight],
        flops=flops_attn,
        name="enc_attn",
    )
    sum_a, sum_b = sum_over_tensor(part_a, part_b)
    hidden_shape = shape((rows, enc_units), LOW)
    part_a, part_b, enc_n2, enc_act, enc_slope = call(
        enc_mlp_kernel,
        [half_rows, half_rows, all_rows, hidden_shape, hidden_shape],
        [
            tok_a, tok_b, sum_a, sum_b, row(enc_out_bias), row(enc_mlp_gain), row(enc_mlp_shift),
            enc_up_weight, row(enc_up_bias), enc_down_weight,
        ],
        flops=flops_mlp,
        name="enc_mlp",
    )
    quarter = rows // 4
    down = add_low(part_a, swap(part_b, "tensor", 1))
    down_x = swap(down[quarter:], "tensor", 2)
    enc_out = (
        tok_a[:quarter].astype(F32)
        + sum_a[:quarter].astype(F32)
        + enc_out_bias
        + down[:quarter].astype(F32)
        + down_x.astype(F32)
        + enc_down_bias
    )
    enc_low = enc_out.astype(LOW)
    enc_low_a, enc_low_b = gather_low(enc_low)

    angles = lax.broadcasted_iota(F32, (patches, dec_width // 2), 0) * jnp.exp(
        lax.broadcasted_iota(F32, (patches, dec_width // 2), 1)
        * (-math.log(10000.0) / (dec_width // 2))
    )
    position = jnp.concatenate([jnp.sin(angles), jnp.cos(angles)], 1)
    own_visible = lax.dynamic_slice_in_dim(visible_index, rank * own_chips, own_chips, 0)
    own_cotangent = lax.dynamic_slice_in_dim(cotangent, rank * own_chips, own_chips, 0)
    small = (
        proj_weight,
        row(proj_bias),
        row(mask_token),
        [
            row(v)
            for v in (
                dec_attn_gain, dec_attn_shift, dec_out_bias, dec_mlp_gain, dec_mlp_shift,
                dec_down_bias,
            )
        ],
    )
    (
        decoded_keep, decoded_send, grad_latent, dec_n1, dec_n2, dec_gml, dec_act, dec_hid,
        dec_gqkv, dec_mixed, dec_vec, dec_upvec,
    ) = dec_call(
        place, enc_low.reshape(own_chips, length, enc_width), small, position, own_visible,
        up_bias_parts, weights, own_cotangent,
    )
    lat_a, lat_b = gather_low(grad_latent.reshape(own_chips * length, dec_width))

    wide_rows = shape((rows // 2, enc_width), F32)
    vec_shape = shape((8, enc_width), F32)
    part_a, part_b, out_a, out_b, enc_gol, enc_hid, vec_mlp = call(
        enc_mlp_back_kernel,
        [half_rows, half_rows, wide_rows, wide_rows, all_rows, hidden_shape, vec_shape],
        [lat_a, lat_b, proj_weight, enc_slope, enc_up_weight, enc_down_weight],
        flops=flops_mlp,
        name="enc_mlp_back",
    )
    back_a, back_b = sum_over_tensor(part_a, part_b)

    saved = (
        dec_n1, dec_n2, dec_gml, own_cotangent.reshape(-1, dec_width), dec_act, dec_hid, dec_gqkv,
        dec_mixed,
    )
    dec_send = dec_weights(place, saved, (dec_vec, dec_upvec), blocks, 1)
    dec_keep = dec_weights(place, saved, (dec_vec, dec_upvec), blocks, 0)
    dec_sum = add_low(dec_keep, swap(dec_send, "tensor", 1))
    dec_sum = add_low(dec_sum[0], swap(dec_sum[1], "tensor", 2))
    dec_share = dp_steps(dec_sum[: blocks // 2], dec_sum[blocks // 2 :])

    enc_piece = enc_width // blocks
    enc_rows = -(-enc_piece // 16) * 16
    proj_own = dec_width // parts
    bundle = shape((blocks // 2, enc_rows, 2 * enc_units + proj_own), LOW)
    mlp_keep, mlp_send = call(
        enc_mlp_weights_kernel,
        [bundle, bundle],
        [enc_n2, enc_hid, enc_gol, enc_act, lat_a, lat_b, enc_low_a, enc_low_b],
        scalars=[place],
        flops=flops_mlp,
        name="enc_mlp_weights",
    )
    mlp_share = dp_steps(mlp_keep, mlp_send)

    part_a, part_b, mid_a, mid_b, enc_gml, enc_gqkv, vec_attn = call(
        functools.partial(enc_attn_back_kernel, length=length),
        [
            half_rows, half_rows, wide_rows, wide_rows, all_rows,
            shape((rows, 3 * enc_inner), LOW), vec_shape,
        ],
        [
            tok_a, tok_b, sum_a, sum_b, row(enc_out_bias), row(enc_mlp_gain), out_a, out_b,
            back_a, back_b, enc_qkv, qkv_w, enc_out_weight,
        ],
        flops=2 * flops_attn,
        name="enc_attn_back",
    )
    grad_a, grad_b = sum_over_tensor(part_a, part_b)
    bundle = shape((blocks // 2, enc_rows + VEC_ROWS, 4 * enc_inner), LOW)
    attn_keep, attn_send = call(
        enc_attn_weights_kernel,
        [bundle, bundle],
        [enc_n1, enc_gqkv, enc_gml, enc_mixed, vec_mlp, vec_attn],
        scalars=[place],
        flops=flops_attn,
        name="enc_attn_weights",
    )
    attn_share = dp_steps(attn_keep, attn_send)

    def in_steps(first, second):
        return jnp.concatenate([first, second], 0).reshape(chips, length, enc_width)

    band_grad = band_grad_call(
        place, band_counts, in_steps(tok_a, tok_b), in_steps(grad_a, grad_b),
        in_steps(mid_a, mid_b), row(enc_attn_gain), visible_index, band_patches.shape, own_chips,
    )

    got = swap(decoded_send, "tensor", 1)
    got_x = swap(jnp.stack([decoded_keep[1], got[1]]), "tensor", 2)
    decoded = to_absolute(jnp.stack([jnp.stack([decoded_keep[0], got[0]]), got_x]), rank)
    decoded = decoded.astype(F32).reshape(chips, patches, -1)

    proj_low = mlp_share[:enc_piece, 2 * enc_units :].astype(LOW)
    proj_core = jnp.stack([proj_low, swap(proj_low, "tensor", 1)])
    proj_all = to_absolute(jnp.stack([proj_core, swap(proj_core, "tensor", 2)]), rank)
    proj_all = proj_all.reshape(parts, enc_piece, proj_own).transpose(1, 0, 2)
    enc_vec = attn_share[enc_rows:, :enc_piece]
    norm_vec = enc_vec[11:13]
    norm_vec = norm_vec + swap(norm_vec, "tensor", 1)
    norm_vec = norm_vec + swap(norm_vec, "tensor", 2)
    enc_qkv_grad = attn_share[:enc_piece, : 3 * enc_inner].T.reshape(3, enc_inner, enc_piece)
    dec_piece = dec_width // blocks
    dec_qkv_grad = dec_share[:dec_piece, 2 * dec_units : 2 * dec_units + dec_kinds].T
    dec_vecs = dec_share[-VEC_ROWS:, :dec_piece]
    return (
        decoded,
        band_grad,
        norm_vec[0],
        norm_vec[1],
        enc_qkv_grad,
        attn_share[:enc_piece, 3 * enc_inner :].T,
        enc_vec[10],
        enc_vec[8],
        enc_vec[9],
        mlp_share[:enc_piece, :enc_units],
        enc_vec[1],
        mlp_share[:enc_piece, enc_units : 2 * enc_units].T,
        enc_vec[0],
        proj_all.reshape(enc_piece, dec_width).astype(F32),
        dec_vecs[6],
        dec_vecs[7],
        dec_vecs[0],
        dec_vecs[1],
        dec_qkv_grad.reshape(3, dec_kinds // 3, dec_piece),
        dec_share[:dec_piece, 2 * dec_units + dec_kinds :].T,
        dec_vecs[2],
        dec_vecs[3],
        dec_vecs[4],
        dec_share[:dec_piece, :dec_units],
        dec_vecs[8],
        dec_share[:dec_piece, dec_units : 2 * dec_units].T,
        dec_vecs[5],
    )


def solution(mesh):
    in_specs = (
        P("dp", None, "tensor", None),
        P("dp"),
        P("dp", None),
        P(),
        P(),
        P(None, "tensor", None),
        P("tensor", None),
        P(),
        P(),
        P(),
        P(None, "tensor"),
        P("tensor"),
        P("tensor", None),
        P(),
        P(),
        P(),
        P(),
        P(),
        P(),
        P(None, "tensor", None),
        P("tensor", None),
        P(),
        P(),
        P(),
        P(None, "tensor"),
        P(),
        P("tensor", None),
        P(),
        P("dp", None, None),
    )
    out_specs = (
        P("dp", None, "tensor"),
        P("dp", None, "tensor", None),
        P("dp"),
        P("dp"),
        P(None, "tensor", "dp"),
        P("tensor", "dp"),
        P("dp"),
        P("dp"),
        P("dp"),
        P("dp", "tensor"),
        P(("tensor", "dp")),
        P("tensor", "dp"),
        P("dp"),
        P("dp", None),
        P("dp"),
        P("dp"),
        P("dp"),
        P("dp"),
        P(None, "tensor", "dp"),
        P("tensor", "dp"),
        P("dp"),
        P("dp"),
        P("dp"),
        P("dp", "tensor"),
        P(("tensor", "dp")),
        P("tensor", "dp"),
        P("dp"),
    )
    return jax.shard_map(body, mesh=mesh, in_specs=in_specs, out_specs=out_specs, check_vma=False)
```

time: 1290 us -> 307 us (0.24); the launches traced: 1270 us -> 306 us
  waiting for transfers between devices: 744 us -> 147 us
  local copies, waits for them, and re-layouts: 279 us -> 16.5 us
  matrix products: 101 us -> 0 us
  Pallas kernels: 0 us -> 89.2 us
  other arithmetic: 92.6 us -> 17.1 us
  blocking collectives: 39.1 us -> 0 us
  starting transfers between devices: 2.13 us -> 34.9 us
  between operations: 16.8 us -> 1.52 us
    psum x7 -> x0, waiting for transfers between devices: 344 us -> none  [the longest x2 127 us: attn_sum(): return lax.psum(partial_out, 'tensor')]
    reduce_scatter x5 -> x0, waiting for transfers between devices: 258 us -> none  [the longest x1 72.5 us: body(): lax.psum_scatter(enc_grads[9], 'dp', scatter_dimension=1, tiled=True)]
    scatter x3 -> x0, local copies, waits for them, and re-layouts: 177 us -> none  [the longest x1 69.8 us: body(): grad_mean = jnp.zeros((chip_count, patches, enc_width), jnp.float32).at[c...]
    ppermute x0 -> x38, waiting for transfers between devices: none -> 147 us  [swap(): return lax.ppermute(values, axis, [(i, i ^ apart) for i in range(size)])]
    unnamed x21 -> x0, waiting for transfers between devices: 111 us -> none
    dot_general x40 -> x0, matrix products: 101 us -> none  [the longest x1 10.1 us: body(): jnp.einsum('cb,cbpd->cpd', band_used.astype(jnp.bfloat16), band_patches,...]
    pallas_call x0 -> x11, Pallas kernels: none -> 89.2 us  [the longest x6 33.2 us: call(): pl.pallas_call(body, out_shape=out_shape, in_specs=specs, out_specs=[pl.B...]
    unnamed x239 -> x88, local copies, waits for them, and re-layouts: 59.9 us -> 6.51 us
  transfers between devices with their start and end apart: 17 -> 38, of which waited for: 14 -> 21; matrix products, arithmetic and copies ran while one was open for 20% -> 8% of each run, Pallas kernels for 0% -> 15%
where the time goes in v1:
time: 307 us; the launch traced here: 306 us
  waiting for transfers between devices  147 us (48%)
  Pallas kernels  89.2 us (29%)
  starting transfers between devices  34.9 us (11%)
  other arithmetic  17.1 us (6%)
  local copies, waits for them, and re-layouts  16.5 us (5%)
    ppermute x38, waiting for transfers between devices, swap(): return lax.ppermute(values, axis, [(i, i ^ apart) for i in range(size)])  147 us
    ppermute x38, starting transfers between devices, swap(): return lax.ppermute(values, axis, [(i, i ^ apart) for i in range(size)])  34.9 us
    pallas_call x6, Pallas kernels, call(): pl.pallas_call(body, out_shape=out_shape, in_specs=specs, out_specs=[pl.B...  33.2 us
    pallas_call x1, Pallas kernels, dec_call(): pl.pallas_call(dec_kernel, grid_spec=pltpu.PrefetchScalarGridSpec(num_sca...  25 us
    pallas_call x2, Pallas kernels, dec_weights(): pl.pallas_call(functools.partial(dec_weights_kernel, first=first), grid_s...  11.4 us
    pallas_call x1, Pallas kernels, band_grad_call(): pl.pallas_call(functools.partial(band_grad_kernel, own_chips=own_chips),...  11.3 us
    pallas_call x1, Pallas kernels, band_mean(): pl.pallas_call(functools.partial(band_mean_kernel, own_chips=own_chips),...  8.31 us
    convert_element_type x11, other arithmetic, add_low(): return (first.astype(F32) + second.astype(F32)).astype(LOW)  8.25 us
  transfers between devices with their start and end apart: 38, of which 21 were waited for; matrix products, arithmetic and copies ran while one was open for 8% of the time, Pallas kernels for 15%

profile of v1, /device:TPU:0, one launch (start us, length us, event | category | flops | bytes accessed | tf_op | source)
XLA Modules:
  0.0 306.5 jit_solution(6285287096057890270)
XLA Ops:
  2.4 8.3 %band_mean.1 = bf16[8,64,768]{2,1,0:T(8,128)(2,1)S(1)} custom-call(s32[2]{0:T(128)S(1)} %pad_add_fusion.place_ref, s32[8]{0:T(128)S(1)} %copy-done.10, bf16[8,13,64,768]{3,2,1,0:T(8,128)(2,1)} %bands_ref.1, s32[8,64,1]{2,1,0:T(8,128)S(1)} %copy.63.visible_ref), custom_call_target="tpu_custom_call" | custom-call | flops 5111808 | bytes 10223616 | tf_op jit(solution)/shard_map/band_mean/pallas_call | solution.py:144
  15.7 9.4 %collective-permute-done.1 = bf16[256,768]{1,0:T(8,128)(2,1)S(1)} collective-permute-done((bf16[256,768]{1,0:T(8,128)(2,1)S(1)}, bf16[256,768]{1,0:T(8,128)(2,1)S(1)}, u32[]{:S(2)}, u32[]{:S(2)}) %collective-permute-start.1) | collective-permute-done | bytes 393248 | tf_op jit(solution)/shard_map/ppermute | solution.py:624
  27.8 5.5 %enc_attn.1 = (bf16[256,768]{1,0:T(8,128)(2,1)S(1)}, bf16[256,768]{1,0:T(8,128)(2,1)S(1)}, bf16[512,768]{1,0:T(8,128)(2,1)}, bf16[512,576]{1,0:T(8,128)(2,1)}, bf16[512,192]{1,0:T(8,128)(2,1)S(1)}) custom-call(bf16[256,768]{1,0:T(8,128)(2,1)S(1)} %bitcast.139, bf16[256,768]{1,0:T(8,128)(2,1)} %copy-done.5, f32[1,768]{1,0:T(1,128)S(1)} %reshape.199.gain, ...), custom_call_target="tpu_custom_call" | custom-call | flops 603979776 | bytes 4331520 | tf_op jit(solution)/shard_map/enc_attn/pallas_call | solution.py:82
  38.5 35.9 %collective-permute-done.4 = bf16[256,768]{1,0:T(8,128)(2,1)} collective-permute-done((bf16[256,768]{1,0:T(8,128)(2,1)}, bf16[256,768]{1,0:T(8,128)(2,1)}, u32[]{:S(2)}, u32[]{:S(2)}) %collective-permute-start.4) | collective-permute-done | bytes 393248 | tf_op jit(solution)/shard_map/ppermute | solution.py:624
  78.1 4.9 %enc_mlp.1 = (bf16[256,768]{1,0:T(8,128)(2,1)S(1)}, bf16[256,768]{1,0:T(8,128)(2,1)S(1)}, bf16[512,768]{1,0:T(8,128)(2,1)}, bf16[512,768]{1,0:T(8,128)(2,1)}, bf16[512,768]{1,0:T(8,128)(2,1)}) custom-call(bf16[256,768]{1,0:T(8,128)(2,1)S(1)} %bitcast.140, bf16[256,768]{1,0:T(8,128)(2,1)S(1)} %copy-done.6, bf16[256,768]{1,0:T(8,128)(2,1)S(1)} %bitcast.146, ...), custom_call_target="tpu_custom_call" | custom-call | flops 1207959552 | bytes 7090176 | tf_op jit(solution)/shard_map/enc_mlp/pallas_call | solution.py:82
  87.8 5.2 %collective-permute-done.7 = bf16[128,768]{1,0:T(8,128)(2,1)S(1)} collective-permute-done((bf16[128,768]{1,0:T(8,128)(2,1)S(1)}, bf16[128,768]{1,0:T(8,128)(2,1)S(1)}, u32[]{:S(2)}, u32[]{:S(2)}) %collective-permute-start.7) | collective-permute-done | bytes 196640 | tf_op jit(solution)/shard_map/ppermute | solution.py:624
  93.2 25.0 %decoder.1 = (bf16[2,2,256,128]{3,2,1,0:T(8,128)(2,1)S(1)}, bf16[2,2,256,128]{3,2,1,0:T(8,128)(2,1)S(1)}, bf16[2,64,512]{2,1,0:T(8,128)(2,1)S(1)}, bf16[512,512]...) custom-call(s32[2]{0:T(128)S(1)} %pad_add_fusion.place_ref, ...), custom_call_target="tpu_custom_call" | custom-call | flops 3221225472 | bytes 16777216 | tf_op jit(solution)/shard_map/decoder/pallas_call | solution.py:535
  123.5 5.6 %dec_weights_0.1 = bf16[2,8,80,1280]{3,2,1,0:T(8,128)(2,1)} custom-call(s32[2]{0:T(128)S(1)} %pad_add_fusion.place_ref, bf16[512,512]{1,0:T(8,128)(2,1)S(1)} %get-tuple-element.98.n1_ref, bf16[512,512]{1,0:T(8,128)(2,1)S(1)} %copy-done.3, bf16[512,512]{1,0:T(8,128)(2,1)S(1)} %copy-done.4, bf16[512,512]{1,0:T(8,128)(2,1)} %bitcast.164, ...), custom_call_target="tpu_custom_call" | custom-call | flops 1342177280 | bytes 8388608 | tf_op jit(solution)/shard_map/dec_weights_0/pallas_call | solution.py:601
  129.1 4.9 %enc_mlp_back.1 = (bf16[256,768]{1,0:T(8,128)(2,1)S(1)}, bf16[256,768]{1,0:T(8,128)(2,1)S(1)}, f32[256,768]{1,0:T(8,128)}, f32[256,768]{1,0:T(8,128)}, bf16[512,...) custom-call(bf16[256,512]{1,0:T(8,128)(2,1)S(1)} %pad_maximum_fusion.8.lat_a, ...), custom_call_target="tpu_custom_call" | custom-call | flops 1207959552 | bytes 8413184 | tf_op jit(solution)/shard_map/enc_mlp_back/pallas_call | solution.py:82
  134.4 5.7 %dec_weights_1.1 = bf16[2,8,80,1280]{3,2,1,0:T(8,128)(2,1)} custom-call(s32[2]{0:T(128)S(1)} %pad_add_fusion.place_ref, bf16[512,512]{1,0:T(8,128)(2,1)S(1)} %get-tuple-element.98.n1_ref, bf16[512,512]{1,0:T(8,128)(2,1)S(1)} %copy-done.3, bf16[512,512]{1,0:T(8,128)(2,1)S(1)} %copy-done.4, bf16[512,512]{1,0:T(8,128)(2,1)} %bitcast.165, ...), custom_call_target="tpu_custom_call" | custom-call | flops 1342177280 | bytes 8388608 | tf_op jit(solution)/shard_map/dec_weights_1/pallas_call | solution.py:601
  142.4 4.6 %collective-permute-done.26 = bf16[128,768]{1,0:T(8,128)(2,1)S(1)} collective-permute-done((bf16[128,768]{1,0:T(8,128)(2,1)S(1)}, bf16[128,768]{1,0:T(8,128)(2,1)S(1)}, u32[]{:S(2)}, u32[]{:S(2)}) %collective-permute-start.26) | collective-permute-done | bytes 196640 | tf_op jit(solution)/shard_map/ppermute | solution.py:624
  149.5 9.7 %collective-permute-done.16 = bf16[256,768]{1,0:T(8,128)(2,1)S(1)} collective-permute-done((bf16[256,768]{1,0:T(8,128)(2,1)S(1)}, bf16[256,768]{1,0:T(8,128)(2,1)S(1)}, u32[]{:S(2)}, u32[]{:S(2)}) %collective-permute-start.16) | collective-permute-done | bytes 393248 | tf_op jit(solution)/shard_map/ppermute | solution.py:624
  159.4 5.0 %collective-permute-done.12 = bf16[2,2,256,128]{3,2,1,0:T(8,128)(2,1)S(1)} collective-permute-done((bf16[2,2,256,128]{3,2,1,0:T(8,128)(2,1)S(1)}, bf16[2,2,256,128]{3,2,1,0:T(8,128)(2,1)S(1)}, u32[]{:S(2)}, u32[]{:S(2)}) %collective-permute-start.12) | collective-permute-done | bytes 262176 | tf_op jit(solution)/shard_map/ppermute | solution.py:624
  164.6 5.3 %enc_mlp_weights.1 = (bf16[4,96,1664]{2,1,0:T(8,128)(2,1)}, bf16[4,96,1664]{2,1,0:T(8,128)(2,1)}) custom-call(s32[2]{0:T(128)S(1)} %pad_add_fusion.place_ref, bf16[512,768]{1,0:T(8,128)(2,1)} %get-tuple-element.92.normed_ref, bf16[512,768]{1,0:T(8,128)(2,1)} %get-tuple-element.93.hidden_ref, bf16[512,768]{1,0:T(8,128)(2,1)} %get-tuple-element.94.low_ref, ...), custom_call_target="tpu_custom_call" | custom-call | flops 1207959552 | bytes 7012352 | tf_op jit(solution)/shard_map/enc_mlp_weights/pallas_call | solution.py:82
  172.4 8.2 %enc_attn_back.1 = (bf16[256,768]{1,0:T(8,128)(2,1)S(1)}, bf16[256,768]{1,0:T(8,128)(2,1)S(1)}, f32[256,768]{1,0:T(8,128)}, f32[256,768]{1,0:T(8,128)}, bf16[512...) custom-call(bf16[256,768]{1,0:T(8,128)(2,1)S(1)} %bitcast.142, bf16[256,768]{1,0:T(8,128)(2,1)S(1)} %copy-done.6, ...), custom_call_target="tpu_custom_call" | custom-call | flops 1207959552 | bytes 9467904 | tf_op jit(solution)/shard_map/enc_attn_back/pallas_call | solution.py:82
  181.7 4.6 %enc_attn_weights.1 = (bf16[4,112,768]{2,1,0:T(8,128)(2,1)S(1)}, bf16[4,112,768]{2,1,0:T(8,128)(2,1)}) custom-call(s32[2]{0:T(128)S(1)} %pad_add_fusion.place_ref, bf16[512,768]{1,0:T(8,128)(2,1)} %get-tuple-element.84.normed_ref, bf16[512,576]{1,0:T(8,128)(2,1)S(1)} %copy-done.7, bf16[512,768]{1,0:T(8,128)(2,1)} %get-tuple-element.86.low_ref, ...), custom_call_target="tpu_custom_call" | custom-call | flops 603979776 | bytes 3784704 | tf_op jit(solution)/shard_map/enc_attn_weights/pallas_call | solution.py:82
  191.0 23.5 %collective-permute-done.21 = bf16[4,112,768]{2,1,0:T(8,128)(2,1)S(1)} collective-permute-done((bf16[4,112,768]{2,1,0:T(8,128)(2,1)}, bf16[4,112,768]{2,1,0:T(8,128)(2,1)S(1)}, u32[]{:S(2)}, u32[]{:S(2)}) %collective-permute-start.21) | collective-permute-done | bytes 688160 | tf_op jit(solution)/shard_map/ppermute | solution.py:624
  218.2 9.4 %collective-permute-done.22 = bf16[2,112,768]{2,1,0:T(8,128)(2,1)S(1)} collective-permute-done((bf16[2,112,768]{2,1,0:T(8,128)(2,1)S(1)}, bf16[2,112,768]{2,1,0:T(8,128)(2,1)S(1)}, u32[]{:S(2)}, u32[]{:S(2)}) %collective-permute-start.22) | collective-permute-done | bytes 344096 | tf_op jit(solution)/shard_map/ppermute | solution.py:624
  235.1 6.0 %collective-permute-done.29 = bf16[2,96,1664]{2,1,0:T(8,128)(2,1)S(1)} collective-permute-done((bf16[2,96,1664]{2,1,0:T(8,128)(2,1)S(1)}, bf16[2,96,1664]{2,1,0:T(8,128)(2,1)S(1)}, u32[]{:S(2)}, u32[]{:S(2)}) %collective-permute-start.29) | collective-permute-done | bytes 639008 | tf_op jit(solution)/shard_map/ppermute | solution.py:624
  244.0 11.3 %band_grad.1 = f32[8,13,64,768]{3,2,1,0:T(8,128)} custom-call(s32[2]{0:T(128)S(1)} %pad_add_fusion.place_ref, s32[8]{0:T(128)S(1)} %copy-done.11, bf16[8,64,768]{2,1,0:T(8,128)(2,1)S(1)} %bitcast.143, bf16[8,64,768]{2,1,0:T(8,128)(2,1)S(1)} %bitcast.144, f32[8,64,768]{2,1,0:T(8,128)} %bitcast.163, f32[1,768]{1,0:T(1,128)S(1)} %reshape.199.gain, ...), custom_call_target="tpu_custom_call" | custom-call | bytes 20447232 | tf_op jit(solution)/shard_map/band_grad/pallas_call | solution.py:347
  261.1 5.2 %collective-permute-done.25 = f32[2,96]{1,0:T(2,128)S(1)} collective-permute-done((f32[2,96]{1,0:T(2,128)S(1)}, f32[2,96]{1,0:T(2,128)S(1)}, u32[]{:S(2)}, u32[]{:S(2)}) %collective-permute-start.25) | collective-permute-done | bytes 800 | tf_op jit(solution)/shard_map/ppermute | solution.py:624
  276.7 6.9 %collective-permute-done.35 = bf16[4,80,1280]{2,1,0:T(8,128)(2,1)S(1)} collective-permute-done((bf16[4,80,1280]{2,1,0:T(8,128)(2,1)S(1)}, bf16[4,80,1280]{2,1,0:T(8,128)(2,1)S(1)}, u32[]{:S(2)}, u32[]{:S(2)}) %collective-permute-start.35) | collective-permute-done | bytes 819232 | tf_op jit(solution)/shard_map/ppermute | solution.py:624
  286.5 8.1 %collective-permute-done.36 = bf16[2,80,1280]{2,1,0:T(8,128)(2,1)S(1)} collective-permute-done((bf16[2,80,1280]{2,1,0:T(8,128)(2,1)S(1)}, bf16[2,80,1280]{2,1,0:T(8,128)(2,1)S(1)}, u32[]{:S(2)}, u32[]{:S(2)}) %collective-permute-start.36) | collective-permute-done | bytes 409632 | tf_op jit(solution)/shard_map/ppermute | solution.py:624
  295.5 8.1 %collective-permute-done.37 = bf16[1,80,1280]{2,1,0:T(8,128)(2,1)S(1)} collective-permute-done((bf16[1,80,1280]{2,1,0:T(8,128)(2,1)S(1)}, bf16[1,80,1280]{2,1,0:T(8,128)(2,1)S(1)}, u32[]{:S(2)}, u32[]{:S(2)}) %collective-permute-start.37) | collective-permute-done | bytes 204832 | tf_op jit(solution)/shard_map/ppermute | solution.py:624
  (234 shorter events, 78.8 us)
Async XLA Ops:
  12.8 12.3 %collective-permute-start.1 = (bf16[256,768]{1,0:T(8,128)(2,1)S(1)}, bf16[256,768]{1,0:T(8,128)(2,1)S(1)}, u32[]{:S(2)}, u32[]{:S(2)}) collective-permute-start(bf16[256,768]{1,0:T(8,128)(2,1)S(1)} %fusion.5), channel_id=1, source_target_pairs={{0,2},{1,3},{2,0},{3,1},{4,6},{5,7},{6,4},{7,5},{8,10},{9,11},{10,... | collective-permute-start | bytes 1179656 | tf_op jit(solution)/shard_map/ppermute | solution.py:624
  34.6 42.1 %collective-permute-start.9 = (bf16[1280,512]{1,0:T(8,128)(2,1)}, bf16[1280,512]{1,0:T(8,128)(2,1)}, u32[]{:S(2)}, u32[]{:S(2)}) collective-permute-start(bf16[1280,512]{1,0:T(8,128)(2,1)} %pad_maximum_fusion.1.w0), channel_id=1, source_target_pairs={{0,2},{1,3},{2,0},{3,1},{4,6},{5,7},{6,4},{7,5},{8,10},{9,11},{10,... | collective-permute-start | bytes 3932168 | tf_op jit(solution)/shard_map/ppermute | solution.py:624
  37.2 37.2 %collective-permute-start.4 = (bf16[256,768]{1,0:T(8,128)(2,1)}, bf16[256,768]{1,0:T(8,128)(2,1)}, u32[]{:S(2)}, u32[]{:S(2)}) collective-permute-start(bf16[256,768]{1,0:T(8,128)(2,1)} %add_convert_fusion.4), channel_id=1, source_target_pairs={{0,2},{1,3},{2,0},{3,1},{4,6},{5,7},{6,4},{7,5},{8,10},{9,11},{10,... | collective-permute-start | bytes 1179656 | tf_op jit(solution)/shard_map/ppermute | solution.py:624
  37.7 55.5 %collective-permute-start.8 = (bf16[1280,512]{1,0:T(8,128)(2,1)}, bf16[1280,512]{1,0:T(8,128)(2,1)}, u32[]{:S(2)}, u32[]{:S(2)}) collective-permute-start(bf16[1280,512]{1,0:T(8,128)(2,1)} %pad_maximum_fusion.1.w0), channel_id=1, source_target_pairs={{0,1},{1,0},{2,3},{3,2},{4,5},{5,4},{6,7},{7,6},{8,9},{9,8},{10,11... | collective-permute-start | bytes 3932168 | tf_op jit(solution)/shard_map/ppermute | solution.py:624
  76.7 16.5 %collective-permute-start.10 = (bf16[1280,512]{1,0:T(8,128)(2,1)}, bf16[1280,512]{1,0:T(8,128)(2,1)}, u32[]{:S(2)}, u32[]{:S(2)}) collective-permute-start(bf16[1280,512]{1,0:T(8,128)(2,1)} %collective-permute-done.9.w2), channel_id=1, source_target_pairs={{0,1},{1,0},{2,3},{3,2},{4,5},{5,4},{6,7},{7,6},{8,9},{9,8},{10,11... | collective-permute-start | bytes 3932168 | tf_op jit(solution)/shard_map/ppermute | solution.py:624
  133.9 13.2 %collective-permute-start.15 = (bf16[256,768]{1,0:T(8,128)(2,1)S(1)}, bf16[256,768]{1,0:T(8,128)(2,1)S(1)}, u32[]{:S(2)}, u32[]{:S(2)}) collective-permute-start(bf16[256,768]{1,0:T(8,128)(2,1)S(1)} %get-tuple-element.78), channel_id=1, source_target_pairs={{0,1},{1,0},{2,3},{3,2},{4,5},{5,4},{6,7},{7,6},{8,9},{9,8},{10,11... | collective-permute-start | bytes 1179656 | tf_op jit(solution)/shard_map/ppermute | solution.py:624
  141.9 87.7 %collective-permute-start.33 = (bf16[2,8,80,1280]{3,2,1,0:T(8,128)(2,1)}, bf16[2,8,80,1280]{3,2,1,0:T(8,128)(2,1)}, u32[]{:S(2)}, u32[]{:S(2)}) collective-permute-start(bf16[2,8,80,1280]{3,2,1,0:T(8,128)(2,1)} %dec_weights_1.1), channel_id=1, source_target_pairs={{0,1},{1,0},{2,3},{3,2},{4,5},{5,4},{6,7},{7,6},{8,9},{9,8},{10,11... | collective-permute-start | bytes 9830408 | tf_op jit(solution)/shard_map/ppermute | solution.py:624
  147.0 17.6 %collective-permute-start.27 = (bf16[256,768]{1,0:T(8,128)(2,1)S(1)}, bf16[256,768]{1,0:T(8,128)(2,1)S(1)}, u32[]{:S(2)}, u32[]{:S(2)}) collective-permute-start(bf16[256,768]{1,0:T(8,128)(2,1)S(1)} %pad_maximum_fusion.6.enc_a), channel_id=1, source_target_pairs={{0,1},{1,0},{2,3},{3,2},{4,5},{5,4},{6,7},{7,6},{8,9},{9,8},{10,11... | collective-permute-start | bytes 1179656 | tf_op jit(solution)/shard_map/ppermute | solution.py:624
  147.2 12.0 %collective-permute-start.16 = (bf16[256,768]{1,0:T(8,128)(2,1)S(1)}, bf16[256,768]{1,0:T(8,128)(2,1)S(1)}, u32[]{:S(2)}, u32[]{:S(2)}) collective-permute-start(bf16[256,768]{1,0:T(8,128)(2,1)S(1)} %add_convert_fusion.2), channel_id=1, source_target_pairs={{0,2},{1,3},{2,0},{3,1},{4,6},{5,7},{6,4},{7,5},{8,10},{9,11},{10,... | collective-permute-start | bytes 1179656 | tf_op jit(solution)/shard_map/ppermute | solution.py:624
  149.1 15.3 %collective-permute-start.12 = (bf16[2,2,256,128]{3,2,1,0:T(8,128)(2,1)S(1)}, bf16[2,2,256,128]{3,2,1,0:T(8,128)(2,1)S(1)}, u32[]{:S(2)}, u32[]{:S(2)}) collective-permute-start(bf16[2,2,256,128]{3,2,1,0:T(8,128)(2,1)S(1)} %pad_maximum_fusion.7), channel_id=1, source_target_pairs={{0,2},{1,3},{2,0},{3,1},{4,6},{5,7},{6,4},{7,5},{8,10},{9,11},{10,... | collective-permute-start | bytes 786440 | tf_op jit(solution)/shard_map/ppermute | solution.py:624
  159.3 12.3 %collective-permute-start.17 = (bf16[256,768]{1,0:T(8,128)(2,1)S(1)}, bf16[256,768]{1,0:T(8,128)(2,1)S(1)}, u32[]{:S(2)}, u32[]{:S(2)}) collective-permute-start(bf16[256,768]{1,0:T(8,128)(2,1)S(1)} %bitcast.166), channel_id=1, source_target_pairs={{0,1},{1,0},{2,3},{3,2},{4,5},{5,4},{6,7},{7,6},{8,9},{9,8},{10,11... | collective-permute-start | bytes 1179656 | tf_op jit(solution)/shard_map/ppermute | solution.py:624
  169.9 46.8 %collective-permute-start.28 = (bf16[4,96,1664]{2,1,0:T(8,128)(2,1)}, bf16[4,96,1664]{2,1,0:T(8,128)(2,1)S(1)}, u32[]{:S(2)}, u32[]{:S(2)}) collective-permute-start(bf16[4,96,1664]{2,1,0:T(8,128)(2,1)} %get-tuple-element.97), channel_id=1, source_target_pairs={{0,4},{4,0},{8,12},{12,8},{16,20},{20,16},{24,28},{28,24},{1,5},{5... | collective-permute-start | bytes 3833864 | tf_op jit(solution)/shard_map/ppermute | solution.py:624
  186.2 28.3 %collective-permute-start.21 = (bf16[4,112,768]{2,1,0:T(8,128)(2,1)}, bf16[4,112,768]{2,1,0:T(8,128)(2,1)S(1)}, u32[]{:S(2)}, u32[]{:S(2)}) collective-permute-start(bf16[4,112,768]{2,1,0:T(8,128)(2,1)} %get-tuple-element.91), channel_id=1, source_target_pairs={{0,4},{4,0},{8,12},{12,8},{16,20},{20,16},{24,28},{28,24},{1,5},{5... | collective-permute-start | bytes 2064392 | tf_op jit(solution)/shard_map/ppermute | solution.py:624
  189.2 28.8 %collective-permute-start.19 = (bf16[256,768]{1,0:T(8,128)(2,1)S(1)}, bf16[256,768]{1,0:T(8,128)(2,1)S(1)}, u32[]{:S(2)}, u32[]{:S(2)}) collective-permute-start(bf16[256,768]{1,0:T(8,128)(2,1)S(1)} %add_convert_fusion.1), channel_id=1, source_target_pairs={{0,2},{1,3},{2,0},{3,1},{4,6},{5,7},{6,4},{7,5},{8,10},{9,11},{10,... | collective-permute-start | bytes 1179656 | tf_op jit(solution)/shard_map/ppermute | solution.py:624
  214.8 12.9 %collective-permute-start.22 = (bf16[2,112,768]{2,1,0:T(8,128)(2,1)S(1)}, bf16[2,112,768]{2,1,0:T(8,128)(2,1)S(1)}, u32[]{:S(2)}, u32[]{:S(2)}) collective-permute-start(bf16[2,112,768]{2,1,0:T(8,128)(2,1)S(1)} %slice.336), channel_id=1, source_target_pairs={{0,8},{4,12},{8,0},{12,4},{16,24},{20,28},{24,16},{28,20},{1,9},{5... | collective-permute-start | bytes 1032200 | tf_op jit(solution)/shard_map/ppermute | solution.py:624
  217.0 24.1 %collective-permute-start.29 = (bf16[2,96,1664]{2,1,0:T(8,128)(2,1)S(1)}, bf16[2,96,1664]{2,1,0:T(8,128)(2,1)S(1)}, u32[]{:S(2)}, u32[]{:S(2)}) collective-permute-start(bf16[2,96,1664]{2,1,0:T(8,128)(2,1)S(1)} %slice.334), channel_id=1, source_target_pairs={{0,8},{4,12},{8,0},{12,4},{16,24},{20,28},{24,16},{28,20},{1,9},{5... | collective-permute-start | bytes 1916936 | tf_op jit(solution)/shard_map/ppermute | solution.py:624
  218.2 25.8 %collective-permute-start.20 = (bf16[256,768]{1,0:T(8,128)(2,1)S(1)}, bf16[256,768]{1,0:T(8,128)(2,1)S(1)}, u32[]{:S(2)}, u32[]{:S(2)}) collective-permute-start(bf16[256,768]{1,0:T(8,128)(2,1)S(1)} %bitcast.168), channel_id=1, source_target_pairs={{0,1},{1,0},{2,3},{3,2},{4,5},{5,4},{6,7},{7,6},{8,9},{9,8},{10,11... | collective-permute-start | bytes 1179656 | tf_op jit(solution)/shard_map/ppermute | solution.py:624
  227.8 27.5 %collective-permute-start.23 = (bf16[1,112,768]{2,1,0:T(8,128)(2,1)S(1)}, bf16[1,112,768]{2,1,0:T(8,128)(2,1)S(1)}, u32[]{:S(2)}, u32[]{:S(2)}) collective-permute-start(bf16[1,112,768]{2,1,0:T(8,128)(2,1)S(1)} %slice.339), channel_id=1, source_target_pairs={{0,16},{4,20},{8,24},{12,28},{16,0},{20,4},{24,8},{28,12},{1,17},{... | collective-permute-start | bytes 516104 | tf_op jit(solution)/shard_map/ppermute | solution.py:624
  233.6 33.2 %collective-permute-start.34 = (bf16[8,80,1280]{2,1,0:T(8,128)(2,1)}, bf16[8,80,1280]{2,1,0:T(8,128)(2,1)}, u32[]{:S(2)}, u32[]{:S(2)}) collective-permute-start(bf16[8,80,1280]{2,1,0:T(8,128)(2,1)} %slice_bitcast_fusion), channel_id=1, source_target_pairs={{0,2},{1,3},{2,0},{3,1},{4,6},{5,7},{6,4},{7,5},{8,10},{9,11},{10,... | collective-permute-start | bytes 4915208 | tf_op jit(solution)/shard_map/ppermute | solution.py:624
  242.1 28.2 %collective-permute-start.30 = (bf16[1,96,1664]{2,1,0:T(8,128)(2,1)}, bf16[1,96,1664]{2,1,0:T(8,128)(2,1)}, u32[]{:S(2)}, u32[]{:S(2)}) collective-permute-start(bf16[1,96,1664]{2,1,0:T(8,128)(2,1)} %slice.337), channel_id=1, source_target_pairs={{0,16},{4,20},{8,24},{12,28},{16,0},{20,4},{24,8},{28,12},{1,17},{... | collective-permute-start | bytes 958472 | tf_op jit(solution)/shard_map/ppermute | solution.py:624
  256.6 9.7 %collective-permute-start.25 = (f32[2,96]{1,0:T(2,128)S(1)}, f32[2,96]{1,0:T(2,128)S(1)}, u32[]{:S(2)}, u32[]{:S(2)}) collective-permute-start(f32[2,96]{1,0:T(2,128)S(1)} %slice_add_fusion.6), channel_id=1, source_target_pairs={{0,2},{1,3},{2,0},{3,1},{4,6},{5,7},{6,4},{7,5},{8,10},{9,11},{10,... | collective-permute-start | bytes 2312 | tf_op jit(solution)/shard_map/ppermute | solution.py:624
  268.7 15.0 %collective-permute-start.35 = (bf16[4,80,1280]{2,1,0:T(8,128)(2,1)S(1)}, bf16[4,80,1280]{2,1,0:T(8,128)(2,1)S(1)}, u32[]{:S(2)}, u32[]{:S(2)}) collective-permute-start(bf16[4,80,1280]{2,1,0:T(8,128)(2,1)S(1)} %slice.266), channel_id=1, source_target_pairs={{0,4},{4,0},{8,12},{12,8},{16,20},{20,16},{24,28},{28,24},{1,5},{5... | collective-permute-start | bytes 2457608 | tf_op jit(solution)/shard_map/ppermute | solution.py:624
  283.9 10.7 %collective-permute-start.36 = (bf16[2,80,1280]{2,1,0:T(8,128)(2,1)S(1)}, bf16[2,80,1280]{2,1,0:T(8,128)(2,1)S(1)}, u32[]{:S(2)}, u32[]{:S(2)}) collective-permute-start(bf16[2,80,1280]{2,1,0:T(8,128)(2,1)S(1)} %slice.335), channel_id=1, source_target_pairs={{0,8},{4,12},{8,0},{12,4},{16,24},{20,28},{24,16},{28,20},{1,9},{5... | collective-permute-start | bytes 1228808 | tf_op jit(solution)/shard_map/ppermute | solution.py:624
  294.7 8.9 %collective-permute-start.37 = (bf16[1,80,1280]{2,1,0:T(8,128)(2,1)S(1)}, bf16[1,80,1280]{2,1,0:T(8,128)(2,1)S(1)}, u32[]{:S(2)}, u32[]{:S(2)}) collective-permute-start(bf16[1,80,1280]{2,1,0:T(8,128)(2,1)S(1)} %slice.338), channel_id=1, source_target_pairs={{0,16},{4,20},{8,24},{12,28},{16,0},{20,4},{24,8},{28,12},{1,17},{... | collective-permute-start | bytes 614408 | tf_op jit(solution)/shard_map/ppermute | solution.py:624
  (57 other events, 597.4 us)
